TPU v7x, 128 devices: a whole 4x4x4 slice. The times are simulated.
128 devices in a mesh: dp: 16 (over z_lo, y, core), ctx: 8 (over x, z_hi).
Axes of the slice: x: 4, y: 4, z: 4 (z_hi: 2, z_lo: 2; z = z_hi * 2 + z_lo), core: 2. Of those that a mesh axis runs over, the one named last changes fastest.
Arguments:
- queries: bfloat16 [16, 8, 384, 4096], P(None, 'ctx', 'dp'), may hold values from -200 to 200
- keys: bfloat16 [16, 8, 384, 512], P(None, 'ctx', 'dp'), may hold values from -6 to 6
- values: bfloat16 [16, 8, 384, 512], P(None, 'ctx', 'dp'), may hold values from -6 to 6
- doc_lengths: int32 [64], replicated, may hold values from 1 to 1152, 49152 in all
Outputs:
- attended: bfloat16 [16, 8, 384, 4096], P(None, 'ctx', 'dp')
Inputs may be any that keep to these rules, and one draw needn't show every extreme that they name: `doc_lengths`: the 64 lengths sum to 49152; the longest is exactly 1152.
All inputs are finite; a program needn't handle non-finite values.
Results may differ from a plain program's by a relative error of at most 0.024.
Values may be sent and summed in bfloat16 or wider, within the bound.
No kernel may reach another device: no remote copies, remote signals or barrier semaphores. Data moves between devices by JAX's collectives and lax.ppermute only.
A program may use at most 128 MiB of HBM per device.

v0:
```python
import jax
import jax.numpy as jnp
from jax import lax
from jax.sharding import PartitionSpec as P

QUERY_HEADS = 32
KEY_VALUE_HEADS = 4
HEAD_WIDTH = 128


rope_theta = 1000000.0


def passed_along(value, axis, steps):
    count = lax.axis_size(axis)
    initial, last = (max(0, -steps), min(count, count - steps))
    return lax.ppermute(value, axis, [(source, source + steps) for source in range(initial, last)])


def rotary_embedding(field, token_positions):
    half_size = field.shape[-1] // 2
    exponent = jnp.arange(half_size, dtype=jnp.float32) * (2.0 / field.shape[-1])
    frequency = jnp.exp(-exponent * jnp.log(jnp.float32(rope_theta)))
    angles = token_positions.astype(jnp.float32)[:, None] * frequency[None, :]
    cosine = jnp.cos(angles)[:, None, :]
    sine = jnp.sin(angles)[:, None, :]
    first = field[..., :half_size].astype(jnp.float32)
    second = field[..., half_size:].astype(jnp.float32)
    turned = jnp.concatenate(
        [first * cosine - second * sine, second * cosine + first * sine], axis=-1
    )
    return turned.astype(jnp.bfloat16)


def doc_index(token_positions, doc_ends):
    return jnp.sum((token_positions[:, None] >= doc_ends[None, :]).astype(jnp.int32), axis=1)


def attend(query_matrix, key_matrix, value_matrix, allowed):
    count_of_rows = query_matrix.shape[0]
    queries_per_group = QUERY_HEADS // KEY_VALUE_HEADS
    grouped_scores = query_matrix.reshape(
        count_of_rows, KEY_VALUE_HEADS, queries_per_group, HEAD_WIDTH
    )
    scale = 1.0 / jnp.sqrt(jnp.float32(HEAD_WIDTH))

    def single_group(index):
        query_part = lax.dynamic_index_in_dim(grouped_scores, index, 1, keepdims=False)
        key_part = lax.dynamic_index_in_dim(key_matrix, index, 1, keepdims=False)
        value_part = lax.dynamic_index_in_dim(value_matrix, index, 1, keepdims=False)
        scores = (
            jnp.einsum("tpd,kd->ptk", query_part, key_part, preferred_element_type=jnp.float32)
            * scale
        )
        scores = jnp.where(allowed[None], scores, -jnp.inf)
        highest = jnp.max(scores, axis=-1, keepdims=True)
        weights = jnp.exp(scores - highest)
        totals = jnp.sum(weights, axis=-1, keepdims=True)
        rounded = weights.astype(jnp.bfloat16)
        return (
            jnp.einsum("ptk,kd->ptd", rounded, value_part, preferred_element_type=jnp.float32)
            / totals
        )

    stacked_heads = lax.map(single_group, jnp.arange(KEY_VALUE_HEADS, dtype=jnp.int32))
    return (
        jnp.transpose(stacked_heads, (2, 0, 1, 3))
        .reshape(count_of_rows, QUERY_HEADS * HEAD_WIDTH)
        .astype(jnp.bfloat16)
    )


def on_device(queries, keys, values, doc_lengths):
    local_queries, block_keys, block_values = (
        lax.all_to_all(queries, "dp", split_axis=0, concat_axis=2, tiled=True),
        lax.all_to_all(keys, "dp", split_axis=0, concat_axis=2, tiled=True),
        lax.all_to_all(values, "dp", split_axis=0, concat_axis=2, tiled=True),
    )
    count_of_rows = local_queries.shape[2]
    block_index = lax.axis_index("dp") * lax.axis_size("ctx") + lax.axis_index("ctx")
    token_positions = block_index * count_of_rows + jnp.arange(count_of_rows, dtype=jnp.int32)
    doc_ends = jnp.cumsum(doc_lengths, dtype=jnp.int32)
    query_matrix = rotary_embedding(
        local_queries.reshape(count_of_rows, QUERY_HEADS, HEAD_WIDTH), token_positions
    )
    key_matrix = rotary_embedding(
        block_keys.reshape(count_of_rows, KEY_VALUE_HEADS, HEAD_WIDTH), token_positions
    ).reshape(count_of_rows, KEY_VALUE_HEADS * HEAD_WIDTH)
    value_matrix = block_values.reshape(count_of_rows, KEY_VALUE_HEADS * HEAD_WIDTH)
    earlier = []
    current = (key_matrix, value_matrix)
    for step_number in range(3):
        current = passed_along((current[0], current[1]), ("dp", "ctx"), 1)
        earlier.insert(0, current)
    gathered_keys = jnp.concatenate([couple[0] for couple in earlier] + [key_matrix], axis=0)
    gathered_values = jnp.concatenate([couple[1] for couple in earlier] + [value_matrix], axis=0)
    key_positions = (block_index - 3) * count_of_rows + jnp.arange(
        4 * count_of_rows, dtype=jnp.int32
    )
    same_doc = (
        doc_index(token_positions, doc_ends)[:, None] == doc_index(key_positions, doc_ends)[None, :]
    )
    allowed = (
        same_doc
        & (key_positions[None, :] <= token_positions[:, None])
        & (key_positions[None, :] >= 0)
    )
    mixed = attend(
        query_matrix,
        gathered_keys.reshape(4 * count_of_rows, KEY_VALUE_HEADS, HEAD_WIDTH),
        gathered_values.reshape(4 * count_of_rows, KEY_VALUE_HEADS, HEAD_WIDTH),
        allowed,
    )
    return lax.all_to_all(
        mixed.reshape(1, 1, count_of_rows, QUERY_HEADS * HEAD_WIDTH),
        "dp",
        split_axis=2,
        concat_axis=0,
        tiled=True,
    )


def solution(mesh):
    in_specs = (
        P(None, "ctx", "dp", None),
        P(None, "ctx", "dp", None),
        P(None, "ctx", "dp", None),
        P(),
    )
    out_specs = P(None, "ctx", "dp", None)
    return jax.shard_map(
        on_device, mesh=mesh, in_specs=in_specs, out_specs=out_specs, check_vma=False
    )
```

profile of v0, /device:TPU:1, one launch (start us, length us, event | category | flops | bytes accessed | tf_op | source)
XLA Modules:
  0.0 392.2 jit_solution(7448425979015057403)
XLA Ops:
  0.0 15.7 %all_to_all.19 = bf16[16,1,24,512]{3,2,1,0:T(8,128)(2,1)} all-to-all(bf16[16,1,24,512]{3,2,1,0:T(8,128)(2,1)} %param.7), channel_id=1, replica_groups=mesh['dp'=16,'ctx'=8] {'dp'}, dimensions={0} | all-to-all | bytes 786432 | tf_op jit(solution)/shard_map/all_to_all | solution.py:76
  15.7 13.5 %all_to_all.40 = bf16[16,1,24,512]{3,2,1,0:T(8,128)(2,1)} all-to-all(bf16[16,1,24,512]{3,2,1,0:T(8,128)(2,1)} %param.8), channel_id=1, replica_groups=mesh['dp'=16,'ctx'=8] {'dp'}, dimensions={0} | all-to-all | bytes 786432 | tf_op jit(solution)/shard_map/all_to_all | solution.py:77
  29.2 4.6 %all-to-all-start.1 = ((bf16[16,1,24,4096]{3,2,1,0:T(8,128)(2,1)}), bf16[16,1,24,4096]{3,2,1,0:T(8,128)(2,1)S(1)}, u32[]{:S(2)}, u32[]{:S(2)}) async-start(bf16[16,1,24,4096]{3,2,1,0:T(8,128)(2,1)} %param.6), calls=%async_computation.1 | async-start | bytes 6291456 | tf_op jit(solution)/shard_map/all_to_all | solution.py:75
  33.8 1.5 multiply_cosine_fusion
  36.4 1.7 fusion.25
  39.6 5.2 %collective-permute-start = (bf16[384,512]{0,1:T(8,128)(2,1)}, bf16[384,512]{0,1:T(8,128)(2,1)}, u32[]{:S(2)}, u32[]{:S(2)}) collective-permute-start(bf16[384,512]{0,1:T(8,128)(2,1)} %bitcast.84), channel_id=1, source_target_pairs={{0,1},{1,2},{2,3},{3,4},{4,5},{5,6},{6,7},{7,8},{8,9},{9,10},{10,1... | collective-permute-start | bytes 1179656 | tf_op jit(solution)/shard_map/ppermute | solution.py:17
  44.8 2.5 collective-permute-start.3
  47.3 29.1 %collective-permute-done = bf16[384,512]{0,1:T(8,128)(2,1)} collective-permute-done((bf16[384,512]{0,1:T(8,128)(2,1)}, bf16[384,512]{0,1:T(8,128)(2,1)}, u32[]{:S(2)}, u32[]{:S(2)}) %collective-permute-start) | collective-permute-done | bytes 393248 | tf_op jit(solution)/shard_map/ppermute | solution.py:17
  76.4 5.6 %collective-permute-start.1 = (bf16[384,512]{0,1:T(8,128)(2,1)}, bf16[384,512]{0,1:T(8,128)(2,1)}, u32[]{:S(2)}, u32[]{:S(2)}) collective-permute-start(bf16[384,512]{0,1:T(8,128)(2,1)} %collective-permute-done), channel_id=1, source_target_pairs={{0,1},{1,2},{2,3},{3,4},{4,5},{5,6},{6,7},{7,8},{8,9},{9,10},{10,1... | collective-permute-start | bytes 1179656 | tf_op jit(solution)/shard_map/ppermute | solution.py:17
  82.0 2.8 collective-permute-done.3
  84.8 5.6 %collective-permute-start.4 = (bf16[384,512]{1,0:T(8,128)(2,1)}, bf16[384,512]{1,0:T(8,128)(2,1)}, u32[]{:S(2)}, u32[]{:S(2)}) collective-permute-start(bf16[384,512]{1,0:T(8,128)(2,1)} %collective-permute-done.3), channel_id=1, source_target_pairs={{0,1},{1,2},{2,3},{3,4},{4,5},{5,6},{6,7},{7,8},{8,9},{9,10},{10,1... | collective-permute-start | bytes 1179656 | tf_op jit(solution)/shard_map/ppermute | solution.py:17
  90.4 4.5 %collective-permute-done.1 = bf16[384,512]{0,1:T(8,128)(2,1)} collective-permute-done((bf16[384,512]{0,1:T(8,128)(2,1)}, bf16[384,512]{0,1:T(8,128)(2,1)}, u32[]{:S(2)}, u32[]{:S(2)}) %collective-permute-start.1) | collective-permute-done | bytes 393248 | tf_op jit(solution)/shard_map/ppermute | solution.py:17
  94.9 3.9 %collective-permute-start.2 = (bf16[384,512]{0,1:T(8,128)(2,1)}, bf16[384,512]{0,1:T(8,128)(2,1)}, u32[]{:S(2)}, u32[]{:S(2)}) collective-permute-start(bf16[384,512]{0,1:T(8,128)(2,1)} %collective-permute-done.1), channel_id=1, source_target_pairs={{0,1},{1,2},{2,3},{3,4},{4,5},{5,6},{6,7},{7,8},{8,9},{9,10},{10,1... | collective-permute-start | bytes 1179656 | tf_op jit(solution)/shard_map/ppermute | solution.py:17
  103.8 3.6 collective-permute-start.5
  108.0 1.8 concatenate.45
  109.9 2.0 copy.68
  111.9 2.0 copy.62
  113.8 1.9 copy.67
  115.8 1.9 copy.61
  117.7 1.9 copy.66
  119.7 2.0 copy.60
  121.6 8.1 %pad_maximum_fusion.1 = bf16[1536,4,128]{2,1,0:T(4,128)(2,1)S(1)} fusion(bf16[384,4,128]{2,1,0:T(4,128)(2,1)S(1)} %maximum_convert_fusion, bf16[384,4,128]{2,1,0:T(4,128)(2,1)} %copy.62, bf16[384,4,128]{2,1,0:T(4,128)(2,1)} %copy.61, bf16[384,4,128]{2,1,0:T(4,128)(2,1)} %copy.60), kind=kLoop, calls=%fused_computation.31 | loop fusion | flops 2359296 | bytes 3145728 | tf_op jit(solution)/shard_map/concatenate | solution.py:95
  131.1 1.9 copy.65
  133.1 2.5 pad_maximum_fusion.2
  137.9 2.8 fusion.22
  140.7 3.4 pad_maximum_fusion
  144.2 141.0 %while.11 = (s32[]{:T(128)}, bf16[4,8,384,128]{2,3,1,0:T(8,128)(2,1)}, s32[4]{0:T(128)S(1)}, bf16[1536,4,128]{2,0,1:T(8,128)(2,1)}, bf16[384,4,8,128]{3,0,2,1:T(...) while((s32[]{:T(128)}, ...), condition=%wide.region_6.7_spmd.clone, body=%wide.region_3.6_spmd.clone.sunk | while | flops 2470963200 | bytes 64567476 | solution.py:65
  146.9 1.5 and_and_fusion.2
  148.4 10.5 %fusion.35 = (f32[8,384]{1,0:T(8,128)S(1)}, f32[1536,384,8]{1,0,2:T(8,128)}) fusion(pred[384,1536]{0,1:T(8,128)(4,1)S(1)} %and_and_fusion.2, bf16[384,4,8,128]{3,0,2,1:T(8,128)(2,1)} %get-tuple-element.251, s32[]{:T(128)S(6)} %select_n.30, bf16[1536,4,128]{2,0,1:T(8,128)(2,1)} %get-tuple-element.250), kind=kOutput, calls=%fused_computation.5.clone.1 | convolution fusion | flops 1222112256 | bytes 20657152 | tf_op jit(solution)/shard_map/while/body/eval_jaxpr/tpd,kd->ptk/dot_general | solution.py:52
  159.0 10.2 %fusion.36 = f32[8,384]{1,0:T(8,128)S(1)} fusion(f32[1536,384,8]{1,0,2:T(8,128)} %get-tuple-element.217, f32[8,384]{1,0:T(8,128)S(1)} %get-tuple-element.218, pred[384,1536]{0,1:T(8,128)(4,1)S(1)} %and_and_fusion.2), kind=kLoop, calls=%fused_computation.3.clone.1 | loop fusion | flops 18871296 | bytes 19488768 | tf_op jit(solution)/shard_map/while/body/eval_jaxpr/reduce_sum | solution.py:58
  169.1 9.1 %divide_bitcast_fusion.2 = bf16[1,8,384,128]{3,2,1,0:T(8,128)(2,1)S(1)} fusion(f32[1536,384,8]{1,0,2:T(8,128)} %get-tuple-element.217, f32[8,384]{1,0:T(8,128)S(1)} %get-tuple-element.218, pred[384,1536]{0,1:T(8,128)(4,1)S(1)} %and_and_fusion.2, f32[8,384]{1,0:T(8,128)S(1)} %fusion.36, bf16[1536,4,128]{0,2,1:T(8,128)(2,1)} %get-tuple-element.252, ...), kind=kOutput, calls=%fused_computation.9.clone.1 | convolution fusion | flops 1227620352 | bytes 20668420 | tf_op jit(solution)/shard_map/while/body/eval_jaxpr/ptk,kd->ptd/dot_general | solution.py:61
  182.1 1.5 and_and_fusion.2
  183.6 10.5 %fusion.35 = (f32[8,384]{1,0:T(8,128)S(1)}, f32[1536,384,8]{1,0,2:T(8,128)}) fusion(pred[384,1536]{0,1:T(8,128)(4,1)S(1)} %and_and_fusion.2, bf16[384,4,8,128]{3,0,2,1:T(8,128)(2,1)} %get-tuple-element.251, s32[]{:T(128)S(6)} %select_n.30, bf16[1536,4,128]{2,0,1:T(8,128)(2,1)} %get-tuple-element.250), kind=kOutput, calls=%fused_computation.5.clone.1 | convolution fusion | flops 1222112256 | bytes 20657152 | tf_op jit(solution)/shard_map/while/body/eval_jaxpr/tpd,kd->ptk/dot_general | solution.py:52
  194.2 10.2 %fusion.36 = f32[8,384]{1,0:T(8,128)S(1)} fusion(f32[1536,384,8]{1,0,2:T(8,128)} %get-tuple-element.217, f32[8,384]{1,0:T(8,128)S(1)} %get-tuple-element.218, pred[384,1536]{0,1:T(8,128)(4,1)S(1)} %and_and_fusion.2), kind=kLoop, calls=%fused_computation.3.clone.1 | loop fusion | flops 18871296 | bytes 19488768 | tf_op jit(solution)/shard_map/while/body/eval_jaxpr/reduce_sum | solution.py:58
  204.3 9.1 %divide_bitcast_fusion.2 = bf16[1,8,384,128]{3,2,1,0:T(8,128)(2,1)S(1)} fusion(f32[1536,384,8]{1,0,2:T(8,128)} %get-tuple-element.217, f32[8,384]{1,0:T(8,128)S(1)} %get-tuple-element.218, pred[384,1536]{0,1:T(8,128)(4,1)S(1)} %and_and_fusion.2, f32[8,384]{1,0:T(8,128)S(1)} %fusion.36, bf16[1536,4,128]{0,2,1:T(8,128)(2,1)} %get-tuple-element.252, ...), kind=kOutput, calls=%fused_computation.9.clone.1 | convolution fusion | flops 1227620352 | bytes 20668420 | tf_op jit(solution)/shard_map/while/body/eval_jaxpr/ptk,kd->ptd/dot_general | solution.py:61
  217.3 1.5 and_and_fusion.2
  218.8 10.5 %fusion.35 = (f32[8,384]{1,0:T(8,128)S(1)}, f32[1536,384,8]{1,0,2:T(8,128)}) fusion(pred[384,1536]{0,1:T(8,128)(4,1)S(1)} %and_and_fusion.2, bf16[384,4,8,128]{3,0,2,1:T(8,128)(2,1)} %get-tuple-element.251, s32[]{:T(128)S(6)} %select_n.30, bf16[1536,4,128]{2,0,1:T(8,128)(2,1)} %get-tuple-element.250), kind=kOutput, calls=%fused_computation.5.clone.1 | convolution fusion | flops 1222112256 | bytes 20657152 | tf_op jit(solution)/shard_map/while/body/eval_jaxpr/tpd,kd->ptk/dot_general | solution.py:52
  229.3 10.2 %fusion.36 = f32[8,384]{1,0:T(8,128)S(1)} fusion(f32[1536,384,8]{1,0,2:T(8,128)} %get-tuple-element.217, f32[8,384]{1,0:T(8,128)S(1)} %get-tuple-element.218, pred[384,1536]{0,1:T(8,128)(4,1)S(1)} %and_and_fusion.2), kind=kLoop, calls=%fused_computation.3.clone.1 | loop fusion | flops 18871296 | bytes 19488768 | tf_op jit(solution)/shard_map/while/body/eval_jaxpr/reduce_sum | solution.py:58
  239.5 9.1 %divide_bitcast_fusion.2 = bf16[1,8,384,128]{3,2,1,0:T(8,128)(2,1)S(1)} fusion(f32[1536,384,8]{1,0,2:T(8,128)} %get-tuple-element.217, f32[8,384]{1,0:T(8,128)S(1)} %get-tuple-element.218, pred[384,1536]{0,1:T(8,128)(4,1)S(1)} %and_and_fusion.2, f32[8,384]{1,0:T(8,128)S(1)} %fusion.36, bf16[1536,4,128]{0,2,1:T(8,128)(2,1)} %get-tuple-element.252, ...), kind=kOutput, calls=%fused_computation.9.clone.1 | convolution fusion | flops 1227620352 | bytes 20668420 | tf_op jit(solution)/shard_map/while/body/eval_jaxpr/ptk,kd->ptd/dot_general | solution.py:61
  254.0 10.5 %fusion.35 = (f32[8,384]{1,0:T(8,128)S(1)}, f32[1536,384,8]{1,0,2:T(8,128)}) fusion(pred[384,1536]{0,1:T(8,128)(4,1)S(1)} %and_and_fusion.2, bf16[384,4,8,128]{3,0,2,1:T(8,128)(2,1)} %get-tuple-element.251, s32[]{:T(128)S(6)} %select_n.30, bf16[1536,4,128]{2,0,1:T(8,128)(2,1)} %get-tuple-element.250), kind=kOutput, calls=%fused_computation.5.clone.1 | convolution fusion | flops 1222112256 | bytes 20657152 | tf_op jit(solution)/shard_map/while/body/eval_jaxpr/tpd,kd->ptk/dot_general | solution.py:52
  264.5 10.2 %fusion.36 = f32[8,384]{1,0:T(8,128)S(1)} fusion(f32[1536,384,8]{1,0,2:T(8,128)} %get-tuple-element.217, f32[8,384]{1,0:T(8,128)S(1)} %get-tuple-element.218, pred[384,1536]{0,1:T(8,128)(4,1)S(1)} %and_and_fusion.2), kind=kLoop, calls=%fused_computation.3.clone.1 | loop fusion | flops 18871296 | bytes 19488768 | tf_op jit(solution)/shard_map/while/body/eval_jaxpr/reduce_sum | solution.py:58
  274.7 9.1 %divide_bitcast_fusion.2 = bf16[1,8,384,128]{3,2,1,0:T(8,128)(2,1)S(1)} fusion(f32[1536,384,8]{1,0,2:T(8,128)} %get-tuple-element.217, f32[8,384]{1,0:T(8,128)S(1)} %get-tuple-element.218, pred[384,1536]{0,1:T(8,128)(4,1)S(1)} %and_and_fusion.2, f32[8,384]{1,0:T(8,128)S(1)} %fusion.36, bf16[1536,4,128]{0,2,1:T(8,128)(2,1)} %get-tuple-element.252, ...), kind=kOutput, calls=%fused_computation.9.clone.1 | convolution fusion | flops 1227620352 | bytes 20668420 | tf_op jit(solution)/shard_map/while/body/eval_jaxpr/ptk,kd->ptd/dot_general | solution.py:61
  285.2 14.4 %copy.73 = bf16[1,1,384,4096]{3,1,0,2:T(2,128)(2,1)} copy(bf16[1,1,384,4096]{2,3,1,0:T(8,128)(2,1)} %bitcast.79) | data formatting | bytes 6291456 | tf_op jit(solution)/shard_map/convert_element_type | solution.py:69
  300.1 21.3 %reduce.1 = bf16[384,4096]{1,0:T(8,128)(2,1)} reduce(bf16[384,1,1,4096]{3,2,1,0:T(2,128)(2,1)} %bitcast.74, bf16[]{:T(256)} %broadcast.89), dimensions={1,2}, to_apply=%bitcast.51.reduce_sub_computation | reduce | bytes 6291458
  321.4 6.6 %reshape.166 = bf16[16,2,49152]{2,1,0:T(2,128)(2,1)S(1)} reshape(bf16[384,4096]{1,0:T(8,128)(2,1)} %reduce.1) | data formatting | bytes 6291456
  328.0 44.7 %all_to_all.41 = bf16[16,2,49152]{2,1,0:T(2,128)(2,1)} all-to-all(bf16[16,2,49152]{2,1,0:T(2,128)(2,1)S(1)} %reshape.166), channel_id=1, replica_groups=mesh['dp'=16,'ctx'=8] {'dp'}, dimensions={0} | all-to-all | bytes 6291456 | tf_op jit(solution)/shard_map/all_to_all | solution.py:114
  372.8 11.5 %reshape.167 = bf16[384,1,1,4096]{3,2,1,0:T(2,128)(2,1)} reshape(bf16[16,2,49152]{2,1,0:T(2,128)(2,1)} %all_to_all.41) | data formatting | bytes 6291456
  384.2 8.0 %copy.79 = bf16[1,1,384,4096]{3,2,0,1:T(8,128)(2,1)} copy(bf16[1,1,384,4096]{3,1,0,2:T(2,128)(2,1)} %bitcast.75) | data formatting | bytes 6291456
  (54 shorter events, 21.8 us)
Async XLA Ops:
  29.2 106.4 %all-to-all-start.1 = ((bf16[16,1,24,4096]{3,2,1,0:T(8,128)(2,1)}), bf16[16,1,24,4096]{3,2,1,0:T(8,128)(2,1)S(1)}, u32[]{:S(2)}, u32[]{:S(2)}) async-start(bf16[16,1,24,4096]{3,2,1,0:T(8,128)(2,1)} %param.6), calls=%async_computation.1 | async-start | bytes 6291456 | tf_op jit(solution)/shard_map/all_to_all | solution.py:75
  33.7 65.1 %copy-start.8 = (s32[64]{0:T(128)S(1)}, s32[64]{0:T(128)}, u32[]{:S(2)}) copy-start(s32[64]{0:T(128)} %param.9) | copy-start | bytes 772
  39.6 36.8 %collective-permute-start = (bf16[384,512]{0,1:T(8,128)(2,1)}, bf16[384,512]{0,1:T(8,128)(2,1)}, u32[]{:S(2)}, u32[]{:S(2)}) collective-permute-start(bf16[384,512]{0,1:T(8,128)(2,1)} %bitcast.84), channel_id=1, source_target_pairs={{0,1},{1,2},{2,3},{3,4},{4,5},{5,6},{6,7},{7,8},{8,9},{9,10},{10,1... | collective-permute-start | bytes 1179656 | tf_op jit(solution)/shard_map/ppermute | solution.py:17
  44.8 40.0 %collective-permute-start.3 = (bf16[384,512]{1,0:T(8,128)(2,1)}, bf16[384,512]{1,0:T(8,128)(2,1)}, u32[]{:S(2)}, u32[]{:S(2)}) collective-permute-start(bf16[384,512]{1,0:T(8,128)(2,1)} %bitcast.80), channel_id=1, source_target_pairs={{0,1},{1,2},{2,3},{3,4},{4,5},{5,6},{6,7},{7,8},{8,9},{9,10},{10,1... | collective-permute-start | bytes 1179656 | tf_op jit(solution)/shard_map/ppermute | solution.py:17
  76.4 18.5 %collective-permute-start.1 = (bf16[384,512]{0,1:T(8,128)(2,1)}, bf16[384,512]{0,1:T(8,128)(2,1)}, u32[]{:S(2)}, u32[]{:S(2)}) collective-permute-start(bf16[384,512]{0,1:T(8,128)(2,1)} %collective-permute-done), channel_id=1, source_target_pairs={{0,1},{1,2},{2,3},{3,4},{4,5},{5,6},{6,7},{7,8},{8,9},{9,10},{10,1... | collective-permute-start | bytes 1179656 | tf_op jit(solution)/shard_map/ppermute | solution.py:17
  84.8 19.0 %collective-permute-start.4 = (bf16[384,512]{1,0:T(8,128)(2,1)}, bf16[384,512]{1,0:T(8,128)(2,1)}, u32[]{:S(2)}, u32[]{:S(2)}) collective-permute-start(bf16[384,512]{1,0:T(8,128)(2,1)} %collective-permute-done.3), channel_id=1, source_target_pairs={{0,1},{1,2},{2,3},{3,4},{4,5},{5,6},{6,7},{7,8},{8,9},{9,10},{10,1... | collective-permute-start | bytes 1179656 | tf_op jit(solution)/shard_map/ppermute | solution.py:17
  94.9 24.8 %collective-permute-start.2 = (bf16[384,512]{0,1:T(8,128)(2,1)}, bf16[384,512]{0,1:T(8,128)(2,1)}, u32[]{:S(2)}, u32[]{:S(2)}) collective-permute-start(bf16[384,512]{0,1:T(8,128)(2,1)} %collective-permute-done.1), channel_id=1, source_target_pairs={{0,1},{1,2},{2,3},{3,4},{4,5},{5,6},{6,7},{7,8},{8,9},{9,10},{10,1... | collective-permute-start | bytes 1179656 | tf_op jit(solution)/shard_map/ppermute | solution.py:17
  98.9 3.0 copy-start.3
  101.9 0.5 copy-start.7
  103.8 27.3 %collective-permute-start.5 = (bf16[384,512]{1,0:T(8,128)(2,1)}, bf16[384,512]{1,0:T(8,128)(2,1)}, u32[]{:S(2)}, u32[]{:S(2)}) collective-permute-start(bf16[384,512]{1,0:T(8,128)(2,1)} %collective-permute-done.4), channel_id=1, source_target_pairs={{0,1},{1,2},{2,3},{3,4},{4,5},{5,6},{6,7},{7,8},{8,9},{9,10},{10,1... | collective-permute-start | bytes 1179656 | tf_op jit(solution)/shard_map/ppermute | solution.py:17
  129.7 3.4 copy-start.2
  136.4 1.4 copy-start
  136.4 1.4 copy-start.1
  140.7 3.5 copy-start.4
  140.7 3.5 copy-start.5
  140.7 3.5 copy-start.6
where the time goes:
time: 394 us; the launch traced here: 392 us
  other arithmetic  92.9 us (24%)
  matrix products  78.5 us (20%)
  blocking collectives  73.9 us (19%)
  local copies, waits for them, and re-layouts  71.4 us (18%)
  waiting for transfers between devices  36.3 us (9%)
  starting transfers between devices  31 us (8%)
  loops' own time  7.93 us (2%)
    all_to_all x1, blocking collectives, on_device(): lax.all_to_all(mixed.reshape(1, 1, count_of_rows, QUERY_HEADS * HEAD_WIDT...  44.7 us
    dot_general x4, matrix products, single_group(): jnp.einsum('tpd,kd->ptk', query_part, key_part, preferred_element_type=jn...  42.1 us
    reduce_sum x4, other arithmetic, single_group(): totals = jnp.sum(weights, axis=-1, keepdims=True)  40.7 us
    dot_general x4, matrix products, single_group(): jnp.einsum('ptk,kd->ptd', rounded, value_part, preferred_element_type=jnp...  36.3 us
    ppermute x6, waiting for transfers between devices, passed_along(): lax.ppermute(value, axis, [(source, source + steps) for source in range(i...  36.3 us
    unnamed x24, local copies, waits for them, and re-layouts  29.4 us
    ppermute x6, starting transfers between devices, passed_along(): lax.ppermute(value, axis, [(source, source + steps) for source in range(i...  26.5 us
    unnamed x1, other arithmetic  21.3 us
  transfers between devices with their start and end apart: 7, of which 3 were waited for; matrix products, arithmetic and copies ran while one was open for 10% of the time, Pallas kernels for 0%

commit v1 on v0

v1 whole, which is shorter than its diff:
```python
import jax
import jax.numpy as jnp
from jax import lax
from jax.experimental import pallas as pl
from jax.experimental.pallas import tpu as pltpu
from jax.sharding import Mesh, PartitionSpec as P

QUERY_HEADS = 32
KEY_VALUE_HEADS = 4
HEAD_WIDTH = 128
ROPE_THETA = 1000000.0

PAIR = 768
HALO = 1152
KEYS = HALO + PAIR
HEADS = 16
KV = 2
PER_KV = 8
TILE = 128
WINDOW = 256
STEPS = PAIR // TILE
MOST = (HALO + TILE) // WINDOW
SCALE = 1.4426950408889634 / 128.0**0.5
LOW = -1e30


def rotated(field, cosine, sine):
    wide = field.astype(jnp.float32)
    return (wide * cosine + pltpu.roll(wide, HEAD_WIDTH // 2, 1) * sine).astype(jnp.bfloat16)


def attend_kernel(
    first_ref, q_ref, own_ref, near_ref, far_ref, cos_ref, sin_ref, start_ref, out_ref,
    k_ref, v_ref, bias_ref, qr_ref,
):
    step = pl.program_id(0)

    @pl.when(step == 0)
    def _():
        base = 0
        for ref in (far_ref, near_ref, own_ref):
            rows = ref.shape[0]
            for piece in range(0, rows, TILE):
                here = pl.ds(base + piece, TILE)
                cosine, sine = cos_ref[here, :], sin_ref[here, :]
                for head in range(KV):
                    wide = pl.ds(head * HEAD_WIDTH, HEAD_WIDTH)
                    k_ref[head, here, :] = rotated(ref[pl.ds(piece, TILE), wide], cosine, sine)
                    v_ref[head, here, :HEAD_WIDTH] = ref[
                        pl.ds(piece, TILE), pl.ds((KV + head) * HEAD_WIDTH, HEAD_WIDTH)
                    ]
                    v_ref[head, here, HEAD_WIDTH:] = jnp.ones((TILE, HEAD_WIDTH), jnp.bfloat16)
            base += rows

    here = pl.ds(pl.multiple_of(HALO + step * TILE, TILE), TILE)
    cosine, sine = cos_ref[here, :], sin_ref[here, :]
    for head in range(HEADS):
        qr_ref[head // 2, pl.ds((head % 2) * TILE, TILE), :] = rotated(
            q_ref[:, pl.ds(head * HEAD_WIDTH, HEAD_WIDTH)], cosine, sine
        )
    stop = step * TILE + HALO + TILE
    windows = (stop - first_ref[step] + WINDOW - 1) // WINDOW

    for count in range(1, MOST + 1):

        @pl.when(windows == count)
        def _():
            width = count * WINDOW
            begin = pl.multiple_of(stop - width, TILE)
            span = pl.ds(begin, width)
            place = begin + lax.broadcasted_iota(jnp.int32, (TILE, width), 1)
            row = step * TILE + HALO + lax.broadcasted_iota(jnp.int32, (TILE, width), 0)
            allowed = (place >= start_ref[:, :1]) & (place <= row)
            bias_ref[:, :width] = jnp.where(allowed, 0.0, LOW)

            for group in range(HEADS // 2):
                kv = group // (PER_KV // 2)
                scores = lax.dot_general(
                    qr_ref[group],
                    k_ref[kv, span, :],
                    (((1,), (1,)), ((), ())),
                    preferred_element_type=jnp.float32,
                )
                bias = bias_ref[:, :width]
                scores = (scores.reshape(2, TILE, width) + bias[None]).reshape(2 * TILE, width)
                top = jnp.max(scores, axis=1, keepdims=True)
                weights = jnp.exp2((scores - top) * SCALE).astype(jnp.bfloat16)
                mixed = jnp.dot(weights, v_ref[kv, span, :], preferred_element_type=jnp.float32)
                result = (mixed[:, :HEAD_WIDTH] / mixed[:, HEAD_WIDTH:]).astype(jnp.bfloat16)
                for part in range(2):
                    out_ref[:, pl.ds((2 * group + part) * HEAD_WIDTH, HEAD_WIDTH)] = result[
                        part * TILE : (part + 1) * TILE
                    ]


def attend(first, q, own, near, far, cosine, sine, start):
    whole = lambda shape: pl.BlockSpec(shape, lambda i, f: (0, 0))
    return pl.pallas_call(
        attend_kernel,
        grid_spec=pltpu.PrefetchScalarGridSpec(
            num_scalar_prefetch=1,
            grid=(STEPS,),
            in_specs=[
                pl.BlockSpec((TILE, HEADS * HEAD_WIDTH), lambda i, f: (i, 0)),
                whole((PAIR, 2 * KV * HEAD_WIDTH)),
                whole((PAIR, 2 * KV * HEAD_WIDTH)),
                whole((HALO - PAIR, 2 * KV * HEAD_WIDTH)),
                whole((KEYS, HEAD_WIDTH)),
                whole((KEYS, HEAD_WIDTH)),
                pl.BlockSpec((TILE, 1), lambda i, f: (i, 0)),
            ],
            out_specs=pl.BlockSpec((TILE, HEADS * HEAD_WIDTH), lambda i, f: (i, 0)),
            scratch_shapes=[
                pltpu.VMEM((KV, KEYS, HEAD_WIDTH), jnp.bfloat16),
                pltpu.VMEM((KV, KEYS, 2 * HEAD_WIDTH), jnp.bfloat16),
                pltpu.VMEM((TILE, MOST * WINDOW), jnp.float32),
                pltpu.VMEM((HEADS // 2, 2 * TILE, HEAD_WIDTH), jnp.bfloat16),
            ],
        ),
        out_shape=jax.ShapeDtypeStruct((PAIR, HEADS * HEAD_WIDTH), jnp.bfloat16),
        compiler_params=pltpu.CompilerParams(
            dimension_semantics=("arbitrary",), vmem_limit_bytes=56 * 1024 * 1024
        ),
        cost_estimate=pl.CostEstimate(
            flops=8_000_000_000, bytes_accessed=10_000_000, transcendentals=12_000_000
        ),
        name="attend",
    )(first, q, own, near, far, cosine, sine, start)


def exchange(value):
    return lax.all_to_all(value, ("zh", "dp"), split_axis=0, concat_axis=0, tiled=True)


def halved(value):
    groups, rows, width = value.shape
    return value.reshape(groups, rows, 2, width // 2).transpose(2, 0, 1, 3)


def moved(value, steps):
    count = lax.axis_size("dp") * lax.axis_size("x")
    pairs = [(2 * i + h, 2 * (i + steps) + h) for i in range(count - steps) for h in range(2)]
    return lax.ppermute(value, ("dp", "x", "zh"), pairs)


def on_device(queries, keys, values, doc_lengths):
    groups, _, rows, _ = queries.shape
    k = halved(keys.reshape(groups, rows, -1))
    v = halved(values.reshape(groups, rows, -1))
    own = exchange(jnp.concatenate([k, v], -1).reshape(2 * groups, rows, -1)).reshape(PAIR, -1)
    near = moved(own, 1)
    far = moved(own[PAIR // 2 :], 2)
    q = exchange(halved(queries.reshape(groups, rows, -1)).reshape(2 * groups, rows, -1))

    base = (lax.axis_index("dp") * lax.axis_size("x") + lax.axis_index("x")) * PAIR
    positions = base - HALO + jnp.arange(KEYS, dtype=jnp.int32)
    half = HEAD_WIDTH // 2
    exponent = jnp.arange(half, dtype=jnp.float32) * (2.0 / HEAD_WIDTH)
    frequency = jnp.exp(-exponent * jnp.log(jnp.float32(ROPE_THETA)))
    angles = positions.astype(jnp.float32)[:, None] * frequency[None, :]
    cosine, sine = jnp.cos(angles), jnp.sin(angles)
    cosine = jnp.concatenate([cosine, cosine], -1)
    sine = jnp.concatenate([-sine, sine], -1)

    docs = jnp.arange(doc_lengths.shape[0], dtype=jnp.int32)
    ends = jnp.sum(jnp.where(docs[:, None] <= docs[None, :], doc_lengths[:, None], 0), axis=0)
    mine = positions[HALO:]
    starts = jnp.max(jnp.where(ends[None, :] <= mine[:, None], ends[None, :], 0), axis=1)
    starts = starts - (base - HALO)

    mixed = attend(
        starts[::TILE], q.reshape(PAIR, -1), own, near, far, cosine, sine, starts[:, None]
    )
    back = exchange(mixed.reshape(2 * groups, rows, -1))
    back = back.reshape(2, groups, rows, -1).transpose(1, 2, 0, 3)
    return back.reshape(queries.shape)


def solution(mesh):
    fine = Mesh(mesh.devices.reshape(16, 4, 2), ("dp", "x", "zh"))
    spec = P(None, ("x", "zh"), "dp", None)
    return jax.shard_map(
        on_device, mesh=fine, in_specs=(spec, spec, spec, P()), out_specs=spec, check_vma=False
    )
```

time: 394 us -> 161 us (0.41)
  other arithmetic: 92.9 us -> 7.17 us
  matrix products: 78.5 us -> 0 us
  local copies, waits for them, and re-layouts: 71.4 us -> 22.5 us
  blocking collectives: 73.9 us -> 49.9 us
  Pallas kernels: 0 us -> 18.7 us
  starting transfers between devices: 31 us -> 21.5 us
  loops' own time: 7.93 us -> 0 us
  waiting for transfers between devices: 36.3 us -> 40.5 us
    dot_general x8 -> x0, matrix products: 78.5 us -> none  [the longest x4 42.1 us: single_group(): jnp.einsum('tpd,kd->ptk', query_part, key_part, preferred_element_type=jn...]
    reduce_sum x6 -> x1, other arithmetic: 42.1 us -> 0.09 us  [on_device(): jnp.sum(jnp.where(docs[:, None] <= docs[None, :], doc_lengths[:, None], 0...]
    unnamed x24 -> x6, local copies, waits for them, and re-layouts: 29.4 us -> 1.67 us
    all_to_all x3 -> x1, blocking collectives: 73.9 us -> 49.9 us  [exchange(): lax.all_to_all(value, ('zh', 'dp'), split_axis=0, concat_axis=0, tiled=True)]
    all_to_all x1 -> x2, waiting for transfers between devices: 0.01 us -> 22.8 us  [exchange(): lax.all_to_all(value, ('zh', 'dp'), split_axis=0, concat_axis=0, tiled=True)]
    unnamed x1 -> x0, other arithmetic: 21.3 us -> none
    ppermute x6 -> x2, starting transfers between devices: 26.5 us -> 7.47 us  [moved(): return lax.ppermute(value, ('dp', 'x', 'zh'), pairs)]
    pallas_call x0 -> x1, Pallas kernels: none -> 18.7 us  [attend(): pl.pallas_call(attend_kernel, grid_spec=pltpu.PrefetchScalarGridSpec(num_...]
  transfers between devices with their start and end apart: 7 -> 4, of which waited for: 3 -> 3; matrix products, arithmetic and copies ran while one was open for 10% -> 10% of each run, Pallas kernels for 0% -> 0%
where the time goes in v1:
time: 161 us; the launch traced here: 160 us
  blocking collectives  49.9 us (31%)
  waiting for transfers between devices  40.5 us (25%)
  local copies, waits for them, and re-layouts  22.5 us (14%)
  starting transfers between devices  21.5 us (13%)
  Pallas kernels  18.7 us (12%)
  other arithmetic  7.17 us (4%)
    all_to_all x1, blocking collectives, exchange(): lax.all_to_all(value, ('zh', 'dp'), split_axis=0, concat_axis=0, tiled=True)  49.9 us
    all_to_all x2, waiting for transfers between devices, exchange(): lax.all_to_all(value, ('zh', 'dp'), split_axis=0, concat_axis=0, tiled=True)  22.8 us
    pallas_call x1, Pallas kernels, attend(): pl.pallas_call(attend_kernel, grid_spec=pltpu.PrefetchScalarGridSpec(num_...  18.7 us
    ppermute x2, waiting for transfers between devices, moved(): return lax.ppermute(value, ('dp', 'x', 'zh'), pairs)  17.7 us
    all_to_all x2, starting transfers between devices, exchange(): lax.all_to_all(value, ('zh', 'dp'), split_axis=0, concat_axis=0, tiled=True)  14.1 us
    ppermute x2, starting transfers between devices, moved(): return lax.ppermute(value, ('dp', 'x', 'zh'), pairs)  7.47 us
    another operation x3, local copies, waits for them, and re-layouts, halved(): return value.reshape(groups, rows, 2, width // 2).transpose(2, 0, 1, 3)  6.95 us
    reshape x1, local copies, waits for them, and re-layouts, on_device(): return back.reshape(queries.shape)  3.98 us
  transfers between devices with their start and end apart: 4, of which 3 were waited for; matrix products, arithmetic and copies ran while one was open for 10% of the time, Pallas kernels for 0%

profile of v1, /device:TPU:1, one launch (start us, length us, event | category | flops | bytes accessed | tf_op | source)
XLA Modules:
  0.0 160.4 jit_solution(11488174296680833173)
XLA Ops:
  0.0 1.1 reshape_reshape.11
  1.1 1.1 reshape_reshape.10
  2.2 0.9 pad_maximum_fusion.2
  3.1 1.0 copy.13
  4.1 9.6 %all-to-all-start.1 = ((bf16[32,24,512]{2,1,0:T(8,128)(2,1)}), bf16[32,24,512]{2,1,0:T(8,128)(2,1)}, u32[]{:S(2)}, u32[]{:S(2)}) async-start(bf16[32,24,512]{2,1,0:T(8,128)(2,1)} %bitcast.5), calls=%async_computation.1 | async-start | bytes 1572864 | tf_op jit(solution)/shard_map/all_to_all | solution.py:132
  13.7 4.8 %reshape_reshape.9 = bf16[16,24,2,2048]{3,2,1,0:T(2,128)(2,1)S(1)} reshape(bf16[16,1,24,4096]{3,2,1,0:T(8,128)(2,1)} %param.4) | data formatting | bytes 6291456 | tf_op jit(solution)/shard_map/reshape;reshape | solution.py:137
  18.5 3.0 %copy.12 = bf16[2,16,24,2048]{3,2,1,0:T(8,128)(2,1)} copy(bf16[2,16,24,2048]{3,0,2,1:T(2,128)(2,1)S(1)} %bitcast.21) | data formatting | bytes 6291456 | tf_op jit(solution)/shard_map/transpose | solution.py:137
  21.5 6.5 %all-to-all-done.1 = bf16[32,24,512]{2,1,0:T(8,128)(2,1)} async-done(((bf16[32,24,512]{2,1,0:T(8,128)(2,1)}), bf16[32,24,512]{2,1,0:T(8,128)(2,1)}, u32[]{:S(2)}, u32[]{:S(2)}) %all-to-all-start.1) | async-done | bytes 786464 | tf_op jit(solution)/shard_map/all_to_all | solution.py:132
  28.0 0.0 copy-start.2
  28.0 4.4 %all-to-all-start = ((bf16[32,24,2048]{2,1,0:T(8,128)(2,1)}), bf16[32,24,2048]{2,1,0:T(8,128)(2,1)S(1)}, u32[]{:S(2)}, u32[]{:S(2)}) async-start(bf16[32,24,2048]{2,1,0:T(8,128)(2,1)} %bitcast.1), calls=%async_computation | async-start | bytes 6291456 | tf_op jit(solution)/shard_map/all_to_all | solution.py:132
  32.5 0.0 copy-done.2
  32.5 0.1 select_reduce_fusion.1
  32.6 0.1 select_reduce_fusion
  32.7 0.7 slice.13.first_ref
  33.4 0.9 sub.24.start_ref
  34.3 3.1 %collective-permute-start = (bf16[768,512]{1,0:T(8,128)(2,1)}, bf16[768,512]{1,0:T(8,128)(2,1)}, u32[]{:S(2)}, u32[]{:S(2)}) collective-permute-start(bf16[768,512]{1,0:T(8,128)(2,1)} %bitcast.6.own_ref), channel_id=1, source_target_pairs={{0,2},{1,3},{2,4},{3,5},{4,6},{5,7},{6,8},{7,9},{8,10},{9,11},{10,... | collective-permute-start | bytes 2359304 | tf_op jit(solution)/shard_map/ppermute | solution.py:143
  37.4 3.5 %fusion = (f32[1920,64]{1,0:T(8,128)S(1)}, f32[1920,64]{1,0:T(8,128)S(1)}, f32[1920,64]{1,0:T(8,128)S(1)}) fusion(f32[64]{0:T(128)S(1)} %multiply_exponential_fusion, f32[1920]{0:T(1024)S(1)} %get-tuple-element.9), kind=kLoop, calls=%fused_computation.6 | loop fusion | flops 245760 | bytes 1482496 | tf_op jit(solution)/shard_map/neg | solution.py:163
  40.9 1.0 slice.17
  41.9 4.4 %collective-permute-start.1 = (bf16[384,512]{1,0:T(8,128)(2,1)S(1)}, bf16[384,512]{1,0:T(8,128)(2,1)S(1)}, u32[]{:S(2)}, u32[]{:S(2)}) collective-permute-start(bf16[384,512]{1,0:T(8,128)(2,1)S(1)} %bitcast.26), channel_id=1, source_target_pairs={{0,4},{1,5},{2,6},{3,7},{4,8},{5,9},{6,10},{7,11},{8,12},{9,13},{1... | collective-permute-start | bytes 1179656 | tf_op jit(solution)/shard_map/ppermute | solution.py:143
  46.3 1.3 pad_maximum_fusion.cos_ref
  47.6 1.3 pad_maximum_fusion.1.sin_ref
  48.9 17.7 %collective-permute-done.1.far_ref = bf16[384,512]{1,0:T(8,128)(2,1)S(1)} collective-permute-done((bf16[384,512]{1,0:T(8,128)(2,1)S(1)}, bf16[384,512]{1,0:T(8,128)(2,1)S(1)}, u32[]{:S(2)}, u32[]{:S(2)}) %collective-permute-start.1) | collective-permute-done | bytes 393248 | tf_op jit(solution)/shard_map/ppermute | solution.py:143
  66.6 0.0 copy-start.1
  66.6 0.0 collective-permute-done.near_ref
  66.6 16.3 %all-to-all-done = bf16[32,24,2048]{2,1,0:T(8,128)(2,1)S(1)} async-done(((bf16[32,24,2048]{2,1,0:T(8,128)(2,1)}), bf16[32,24,2048]{2,1,0:T(8,128)(2,1)S(1)}, u32[]{:S(2)}, u32[]{:S(2)}) %all-to-all-start) | async-done | bytes 3145760 | tf_op jit(solution)/shard_map/all_to_all | solution.py:132
  82.9 0.0 copy-start
  82.9 0.0 copy-done.1
  82.9 1.7 %copy-done = bf16[32,24,2048]{2,1,0:T(8,128)(2,1)} copy-done((bf16[32,24,2048]{2,1,0:T(8,128)(2,1)}, bf16[32,24,2048]{2,1,0:T(8,128)(2,1)S(1)}, u32[]{:S(2)}) %copy-start) | copy-done | bytes 3145752
  84.5 18.7 %attend.1 = bf16[768,2048]{1,0:T(8,128)(2,1)} custom-call(s32[6]{0:T(128)} %slice.13.first_ref, bf16[768,2048]{1,0:T(8,128)(2,1)} %bitcast.22, bf16[768,512]{1,0:T(8,128)(2,1)} %bitcast.6.own_ref, bf16[768,512]{1,0:T(8,128)(2,1)} %collective-permute-done.near_ref, bf16[384,512]{1,0:T(8,128)(2,1)} %copy-done.1, f32[1920,128]{1,0:T(8,128)} %pad_maximum_fusion.cos_ref, ...), custom_call_target="tpu_custom_call" | custom-call | flops 8000000000 | bytes 10000000 | tf_op jit(solution)/shard_map/attend/pallas_call | solution.py:98
  103.3 49.9 %all_to_all.15 = bf16[32,24,2048]{2,1,0:T(8,128)(2,1)S(1)} all-to-all(bf16[32,24,2048]{2,1,0:T(8,128)(2,1)} %bitcast.23), channel_id=1, replica_groups=mesh['dp'=16,'x'=4,'zh'=2] {'zh','dp'}, dimensions={0} | all-to-all | bytes 6291456 | tf_op jit(solution)/shard_map/all_to_all | solution.py:132
  153.2 3.3 %copy.17 = bf16[2,16,24,2048]{3,0,2,1:T(2,128)(2,1)S(1)} copy(bf16[2,16,24,2048]{3,2,1,0:T(8,128)(2,1)S(1)} %bitcast.19) | data formatting | bytes 6291456 | tf_op jit(solution)/shard_map/reshape | solution.py:175
  156.4 4.0 %reshape.52 = bf16[16,1,24,4096]{3,2,1,0:T(8,128)(2,1)} reshape(bf16[16,24,2,2048]{3,2,1,0:T(2,128)(2,1)S(1)} %bitcast.20) | data formatting | bytes 6291456 | tf_op jit(solution)/shard_map/reshape | solution.py:176
  (4 shorter events, 0.0 us)
Async XLA Ops:
  4.1 23.9 %all-to-all-start.1 = ((bf16[32,24,512]{2,1,0:T(8,128)(2,1)}), bf16[32,24,512]{2,1,0:T(8,128)(2,1)}, u32[]{:S(2)}, u32[]{:S(2)}) async-start(bf16[32,24,512]{2,1,0:T(8,128)(2,1)} %bitcast.5), calls=%async_computation.1 | async-start | bytes 1572864 | tf_op jit(solution)/shard_map/all_to_all | solution.py:132
  28.0 4.5 %copy-start.2 = (s32[64]{0:T(128)S(1)}, s32[64]{0:T(128)}, u32[]{:S(2)}) copy-start(s32[64]{0:T(128)} %param.7) | copy-start | bytes 772
  28.0 54.8 %all-to-all-start = ((bf16[32,24,2048]{2,1,0:T(8,128)(2,1)}), bf16[32,24,2048]{2,1,0:T(8,128)(2,1)S(1)}, u32[]{:S(2)}, u32[]{:S(2)}) async-start(bf16[32,24,2048]{2,1,0:T(8,128)(2,1)} %bitcast.1), calls=%async_computation | async-start | bytes 6291456 | tf_op jit(solution)/shard_map/all_to_all | solution.py:132
  34.3 32.3 %collective-permute-start = (bf16[768,512]{1,0:T(8,128)(2,1)}, bf16[768,512]{1,0:T(8,128)(2,1)}, u32[]{:S(2)}, u32[]{:S(2)}) collective-permute-start(bf16[768,512]{1,0:T(8,128)(2,1)} %bitcast.6.own_ref), channel_id=1, source_target_pairs={{0,2},{1,3},{2,4},{3,5},{4,6},{5,7},{6,8},{7,9},{8,10},{9,11},{10,... | collective-permute-start | bytes 2359304 | tf_op jit(solution)/shard_map/ppermute | solution.py:143
  41.9 24.6 %collective-permute-start.1 = (bf16[384,512]{1,0:T(8,128)(2,1)S(1)}, bf16[384,512]{1,0:T(8,128)(2,1)S(1)}, u32[]{:S(2)}, u32[]{:S(2)}) collective-permute-start(bf16[384,512]{1,0:T(8,128)(2,1)S(1)} %bitcast.26), channel_id=1, source_target_pairs={{0,4},{1,5},{2,6},{3,7},{4,8},{5,9},{6,10},{7,11},{8,12},{9,13},{1... | collective-permute-start | bytes 1179656 | tf_op jit(solution)/shard_map/ppermute | solution.py:143
  66.6 16.3 %copy-start.1 = (bf16[384,512]{1,0:T(8,128)(2,1)}, bf16[384,512]{1,0:T(8,128)(2,1)S(1)}, u32[]{:S(2)}) copy-start(bf16[384,512]{1,0:T(8,128)(2,1)S(1)} %collective-permute-done.1.far_ref) | copy-start | bytes 1179652
  82.9 1.7 %copy-start = (bf16[32,24,2048]{2,1,0:T(8,128)(2,1)}, bf16[32,24,2048]{2,1,0:T(8,128)(2,1)S(1)}, u32[]{:S(2)}) copy-start(bf16[32,24,2048]{2,1,0:T(8,128)(2,1)S(1)} %all-to-all-done) | copy-start | bytes 9437188

commit v2 on v1

v2 whole, which is shorter than its diff:
```python
import jax
import jax.numpy as jnp
from jax import lax
from jax.experimental import pallas as pl
from jax.experimental.pallas import tpu as pltpu
from jax.sharding import Mesh, PartitionSpec as P

QUERY_HEADS = 32
KEY_VALUE_HEADS = 4
WIDTH = 128
HALF = WIDTH // 2
ROPE_THETA = 1000000.0
GROUPS = 16
ROWS = 24
GROUP = 3072
PAIR = 768
HALO = 1152
FAR = HALO - PAIR
SLOTS = 2
PER_KV = QUERY_HEADS // KEY_VALUE_HEADS
PEERS = 32
PIECE = PER_KV * ROWS
TILE = 96
SOURCES = TILE // ROWS
WINDOW = 256
STEPS = PAIR // TILE
MOST = 5
REACH = MOST * WINDOW
PAD = REACH - HALO - TILE
KEYS = PAD + HALO + PAIR
PARTS = 2
SCALE = 1.4426950408889634 / WIDTH**0.5
LOW = -1e30
MIB = 1024 * 1024

HBM = pl.BlockSpec(memory_space=pltpu.HBM)
VMEM = pl.BlockSpec(memory_space=pltpu.VMEM)
SMEM = pl.BlockSpec(memory_space=pltpu.SMEM)


def resident(value):
    return pltpu.with_memory_space_constraint(value, pltpu.VMEM)


def stored(value):
    return pltpu.with_memory_space_constraint(value, pltpu.HBM)


def small(limit, **rest):
    return dict(compiler_params=pltpu.CompilerParams(vmem_limit_bytes=limit * MIB), **rest)


def rotated(field, cosine, sine):
    wide = field.astype(jnp.float32)
    return wide * cosine + pltpu.roll(wide, HALF, wide.ndim - 1) * sine


def split_keys_kernel(k_ref, v_ref, out_ref, held, sems, out_sems):
    arrivals = []
    for head in range(KEY_VALUE_HEADS):
        for index, ref in enumerate((k_ref, v_ref)):
            arrivals.append(
                pltpu.make_async_copy(
                    ref.at[:, :, pl.ds(head * WIDTH, WIDTH)],
                    held.at[head, :, index],
                    sems.at[head * 2 + index],
                )
            )
    for copy in arrivals:
        copy.start()
    leaves = []
    for head in range(KEY_VALUE_HEADS):
        for copy in arrivals[2 * head : 2 * head + 2]:
            copy.wait()
        leaves.append(pltpu.make_async_copy(held.at[head], out_ref.at[head], out_sems.at[head]))
        leaves[-1].start()
    for copy in leaves:
        copy.wait()


def split_keys(keys, values):
    shape = (KEY_VALUE_HEADS, GROUPS, 2, ROWS, WIDTH)
    return pl.pallas_call(
        split_keys_kernel,
        in_specs=[HBM, HBM],
        out_specs=HBM,
        out_shape=pltpu.HBM(shape, jnp.bfloat16),
        scratch_shapes=[
            pltpu.VMEM(shape, jnp.bfloat16),
            pltpu.SemaphoreType.DMA((2 * KEY_VALUE_HEADS,)),
            pltpu.SemaphoreType.DMA((KEY_VALUE_HEADS,)),
        ],
        **small(8, name="split_keys"),
    )(stored(keys), stored(values))


def split_queries_kernel(q_ref, cos_ref, sin_ref, out_ref, held, made, sems, out_sems):
    chunk = 4
    arrivals, leaves = [], []
    for part in range(GROUPS // chunk):
        here = pl.ds(part * chunk, chunk)
        arrivals.append(pltpu.make_async_copy(q_ref.at[here], held.at[here], sems.at[part]))
        leaves.append(
            pltpu.make_async_copy(made.at[:, here], out_ref.at[:, here], out_sems.at[part])
        )
    for copy in arrivals:
        copy.start()
    for part in range(GROUPS // chunk):
        arrivals[part].wait()

        def one_group(index, _):
            group = part * chunk + index
            cosine, sine = cos_ref[group], sin_ref[group]
            for head in range(QUERY_HEADS):
                turned = rotated(held[group, :, pl.ds(head * WIDTH, WIDTH)], cosine, sine)
                made[head // PER_KV, group, head % PER_KV] = turned.astype(jnp.bfloat16)
            return 0

        lax.fori_loop(0, chunk, one_group, 0)
        leaves[part].start()
    for copy in leaves:
        copy.wait()


def split_queries(queries, cosine, sine):
    shape = (KEY_VALUE_HEADS, GROUPS, PER_KV, ROWS, WIDTH)
    return pl.pallas_call(
        split_queries_kernel,
        in_specs=[HBM, VMEM, VMEM],
        out_specs=HBM,
        out_shape=pltpu.HBM(shape, jnp.bfloat16),
        scratch_shapes=[
            pltpu.VMEM((GROUPS, ROWS, QUERY_HEADS * WIDTH), jnp.bfloat16),
            pltpu.VMEM(shape, jnp.bfloat16),
            pltpu.SemaphoreType.DMA((4,)),
            pltpu.SemaphoreType.DMA((4,)),
        ],
        cost_estimate=pl.CostEstimate(
            flops=10_000_000, bytes_accessed=6_500_000, transcendentals=0
        ),
        **small(16, name="split_queries"),
    )(stored(queries), resident(cosine), resident(sine))


def join_heads_kernel(in_ref, out_ref, held, sems):
    chunk = 4
    copies = []
    for part in range(GROUPS // chunk):

        def one_group(index, _):
            group = part * chunk + index
            for head in range(QUERY_HEADS):
                held[group, :, pl.ds(head * WIDTH, WIDTH)] = in_ref[
                    head // PER_KV, group, head % PER_KV
                ]
            return 0

        lax.fori_loop(0, chunk, one_group, 0)
        here = pl.ds(part * chunk, chunk)
        copies.append(pltpu.make_async_copy(held.at[here], out_ref.at[here], sems.at[part]))
        copies[-1].start()
    for copy in copies:
        copy.wait()


def join_heads(parts):
    return pl.pallas_call(
        join_heads_kernel,
        in_specs=[VMEM],
        out_specs=HBM,
        out_shape=pltpu.HBM((GROUPS, ROWS, QUERY_HEADS * WIDTH), jnp.bfloat16),
        scratch_shapes=[
            pltpu.VMEM((GROUPS, ROWS, QUERY_HEADS * WIDTH), jnp.bfloat16),
            pltpu.SemaphoreType.DMA((4,)),
        ],
        **small(16, name="join_heads"),
    )(resident(parts))


def turn_keys_kernel(in_ref, cos_ref, sin_ref, *out_refs):
    for slot in range(SLOTS):
        own_ref, far_ref = out_refs[slot], out_refs[SLOTS + slot]
        keys = in_ref[:, slot, 0].astype(jnp.float32).reshape(PAIR, WIDTH)
        values = in_ref[:, slot, 1].astype(jnp.float32).reshape(PAIR, WIDTH)
        keys = rotated(keys, cos_ref[slot], sin_ref[slot]).astype(jnp.bfloat16)
        values = values.astype(jnp.bfloat16)
        own_ref[:, :WIDTH] = keys
        own_ref[:, WIDTH:] = values
        far_ref[:, :WIDTH] = keys[PAIR - FAR :]
        far_ref[:, WIDTH:] = values[PAIR - FAR :]


def turn_keys(own, cosine, sine):
    return pl.pallas_call(
        turn_keys_kernel,
        in_specs=[VMEM] * 3,
        out_specs=[VMEM] * 4,
        out_shape=[jax.ShapeDtypeStruct((PAIR, 2 * WIDTH), jnp.bfloat16)] * 2
        + [jax.ShapeDtypeStruct((FAR, 2 * WIDTH), jnp.bfloat16)] * 2,
        **small(12, name="turn_keys"),
    )(stored(own), cosine, sine)


def attend_kernel(
    first_ref, base_ref, flag_ref, ends_ref, q_ref, own0, own1, near0, near1, far0, far1, out_ref,
    q_held, k_ref, v_ref, start_ref, bias_ref, s_ref, p_ref, q_sems, k_sems, v_sems,
):
    size = PARTS * PIECE
    pieces = []
    for place, (pair, base, flag) in enumerate((
        ((own0, own1), PAD + HALO, 0),
        ((near0, near1), PAD + FAR, flag_ref[1]),
        ((far0, far1), PAD, flag_ref[0]),
    )):
        for index, ref in enumerate(pair):
            to = (flag + index) % SLOTS
            rows = pl.ds(base, ref.shape[0])
            for column, (held, sems) in enumerate(((k_ref, k_sems), (v_ref, v_sems))):
                pieces.append(
                    pltpu.make_async_copy(
                        ref.at[:, pl.ds(column * WIDTH, WIDTH)],
                        held.at[to, rows, :],
                        sems.at[place * SLOTS + index],
                    )
                )
    for copy in pieces:
        copy.start()

    def arrival(index):
        slot, step = index // STEPS, index % STEPS
        return pltpu.make_async_copy(
            q_ref.at[pl.ds(step * SOURCES, SOURCES), slot], q_held.at[index], q_sems.at[index]
        )

    for index in range(SLOTS * STEPS):
        arrival(index).start()
    for slot in range(SLOTS):
        k_ref[slot, :PAD, :] = jnp.zeros((PAD, WIDTH), jnp.bfloat16)
        v_ref[slot, :PAD, :] = jnp.zeros((PAD, WIDTH), jnp.bfloat16)
    for index in range(SLOTS * STEPS):
        base = base_ref[index // STEPS]
        ends = jnp.broadcast_to(ends_ref[...] - base, (TILE, WIDTH))
        own = PAD + HALO + index % STEPS * TILE
        own = own + lax.broadcasted_iota(jnp.int32, (TILE, WIDTH), 0)
        start = jnp.max(jnp.where(ends <= own, ends, -base), axis=1, keepdims=True)
        start_ref[index] = jnp.broadcast_to(start, (TILE, WIDTH))
    for copy in pieces:
        copy.wait()

    def one_step(index, _):
        slot, step = index // STEPS, index % STEPS
        stop = step * TILE + REACH
        windows = (stop - first_ref[index] + WINDOW - 1) // WINDOW
        arrival(index).wait()

        for count in range(1, MOST + 1):

            @pl.when(windows == count)
            def _():
                width = count * WINDOW
                begin = pl.multiple_of(stop - width, 32)
                lane = lax.broadcasted_iota(jnp.int32, (TILE, WIDTH), 1)
                row = stop - TILE + lax.broadcasted_iota(jnp.int32, (TILE, WIDTH), 0)
                start = start_ref[index]
                for column in range(0, width, WIDTH):
                    key = lane + (begin + column)
                    allowed = (key >= start) & (key <= row)
                    bias_ref[:, pl.ds(column, WIDTH)] = jnp.where(allowed, 0.0, LOW)

                def score(turn):
                    q = q_held[index, pl.ds(turn * PARTS, PARTS)].reshape(size, WIDTH)
                    rows = pl.ds(turn * PARTS * ROWS, PARTS * ROWS)
                    top = None
                    for window in range(count):
                        here = pl.ds(pl.multiple_of(begin + window * WINDOW, 32), WINDOW)
                        scores = lax.dot_general(
                            q,
                            k_ref[slot, here, :],
                            (((1,), (1,)), ((), ())),
                            preferred_element_type=jnp.float32,
                        )
                        bias = bias_ref[rows, pl.ds(window * WINDOW, WINDOW)]
                        scores = scores.reshape(PARTS, PER_KV, ROWS, WINDOW)
                        scores = scores + bias.reshape(PARTS, 1, ROWS, WINDOW)
                        scores = scores.reshape(size, WINDOW)
                        s_ref[turn, :, pl.ds(window * WINDOW, WINDOW)] = scores
                        high = jnp.maximum(scores[:, :WIDTH], scores[:, WIDTH:])
                        top = high if top is None else jnp.maximum(top, high)
                    return jnp.max(top, axis=1, keepdims=True)

                def weigh(turn, top):
                    total = None
                    for window in range(count):
                        here = pl.ds(window * WINDOW, WINDOW)
                        weights = jnp.exp2((s_ref[turn, :, here] - top) * SCALE)
                        p_ref[turn, :, here] = weights.astype(jnp.bfloat16)
                        both = weights[:, :WIDTH] + weights[:, WIDTH:]
                        total = both if total is None else total + both
                    return jnp.sum(total, axis=1, keepdims=True)

                def mix(turn, total):
                    mixed = jnp.dot(
                        p_ref[turn, :, :width],
                        v_ref[slot, pl.ds(begin, width), :],
                        preferred_element_type=jnp.float32,
                    )
                    result = (mixed / total).astype(jnp.bfloat16)
                    for part in range(PARTS):
                        out_ref[step * SOURCES + turn * PARTS + part, slot] = result[
                            part * PIECE : (part + 1) * PIECE
                        ]

                turns = SOURCES // PARTS
                tops = [score(0)]
                for turn in range(turns):
                    if turn + 1 < turns:
                        tops.append(score(turn + 1))
                    mix(turn, weigh(turn, tops[turn]))

        return 0

    lax.fori_loop(0, SLOTS * STEPS, one_step, 0)


def attend(first, base, flags, ends, q, own, near, far):
    size = PARTS * PIECE
    turns = SOURCES // PARTS
    return pl.pallas_call(
        attend_kernel,
        in_specs=[SMEM] * 3 + [VMEM] + [HBM] * 7,
        out_specs=VMEM,
        out_shape=pltpu.VMEM((PEERS, SLOTS, PIECE, WIDTH), jnp.bfloat16),
        scratch_shapes=[
            pltpu.VMEM((SLOTS * STEPS, SOURCES, PIECE, WIDTH), jnp.bfloat16),
            pltpu.VMEM((SLOTS, KEYS, WIDTH), jnp.bfloat16),
            pltpu.VMEM((SLOTS, KEYS, WIDTH), jnp.bfloat16),
            pltpu.VMEM((SLOTS * STEPS, TILE, WIDTH), jnp.int32),
            pltpu.VMEM((TILE, REACH), jnp.float32),
            pltpu.VMEM((turns, size, REACH), jnp.float32),
            pltpu.VMEM((turns, size, REACH), jnp.bfloat16),
            pltpu.SemaphoreType.DMA((SLOTS * STEPS,)),
            pltpu.SemaphoreType.DMA((3 * SLOTS,)),
            pltpu.SemaphoreType.DMA((3 * SLOTS,)),
        ],
        cost_estimate=pl.CostEstimate(
            flops=8_000_000_000, bytes_accessed=10_000_000, transcendentals=12_000_000
        ),
        **small(24, name="attend"),
    )(first, base, flags, ends, *map(stored, (q,) + own + near + far))


def exchange(value):
    return lax.all_to_all(value, ("zh", "dp"), split_axis=0, concat_axis=0, tiled=True)


def moved(value, slot, steps):
    pairs = []
    for dp in range(16):
        for x in range(4):
            to = dp
            if x + steps >= 4 and slot == 1:
                if dp % 8 == 7:
                    continue
                to = dp + 1
            for h in range(2):
                pairs.append((dp * 8 + x * 2 + h, to * 8 + (x + steps) % 4 * 2 + h))
    return lax.ppermute(value, ("dp", "x", "zh"), pairs)


def tables(positions):
    lane = jnp.arange(WIDTH, dtype=jnp.int32)
    exponent = (lane % HALF).astype(jnp.float32) * (2.0 / WIDTH)
    frequency = jnp.exp(-exponent * jnp.log(jnp.float32(ROPE_THETA)))
    angles = positions.astype(jnp.float32)[..., None] * frequency
    return jnp.cos(angles), jnp.sin(angles) * jnp.where(lane < HALF, -1.0, 1.0)


def on_device(queries, keys, values, doc_lengths):
    dp, x, zh = lax.axis_index("dp"), lax.axis_index("x"), lax.axis_index("zh")
    own = split_keys(keys.reshape(GROUPS, ROWS, -1), values.reshape(GROUPS, ROWS, -1))
    own = exchange(own.reshape(PEERS, SLOTS, 2, ROWS, WIDTH))

    home = (
        jnp.arange(GROUPS, dtype=jnp.int32)[:, None] * GROUP
        + (x * 2 + zh) * (PAIR // 2)
        + dp * ROWS
        + jnp.arange(ROWS, dtype=jnp.int32)[None, :]
    )
    q = split_queries(queries.reshape(GROUPS, ROWS, -1), *tables(home))
    q = exchange(q.reshape(PEERS, SLOTS, PER_KV, ROWS, WIDTH))

    base = (dp % 8 * SLOTS + jnp.arange(SLOTS, dtype=jnp.int32)) * GROUP + x * PAIR
    positions = base[:, None] + jnp.arange(PAIR, dtype=jnp.int32)[None, :]
    own0, own1, last0, last1 = turn_keys(own, *tables(positions))
    near = moved(own0, 0, 1), moved(own1, 1, 1)
    far = moved(last0, 0, 2), moved(last1, 1, 2)
    flags = jnp.stack([(x < 2).astype(jnp.int32), (x < 1).astype(jnp.int32)])

    docs = jnp.arange(WIDTH, dtype=jnp.int32)
    lengths = jnp.pad(doc_lengths, (0, WIDTH - doc_lengths.shape[0]))
    ends = jnp.sum(jnp.where(docs[:, None] <= docs[None, :], lengths[:, None], 0), axis=0)
    heads = base[:, None] + jnp.arange(0, PAIR, TILE, dtype=jnp.int32)[None, :]
    first = jnp.max(jnp.where(ends <= heads[..., None], ends, 0), axis=-1)
    base = base - PAD - HALO

    mixed = attend(
        (first - base[:, None]).reshape(-1),
        base,
        flags,
        ends[None, :],
        q.reshape(PEERS, SLOTS, PIECE, WIDTH),
        (own0, own1),
        near,
        far,
    )
    back = exchange(mixed.reshape(PEERS, SLOTS, PER_KV, ROWS, WIDTH))
    back = join_heads(back.reshape(KEY_VALUE_HEADS, GROUPS, PER_KV, ROWS, WIDTH))
    return back.reshape(queries.shape)


def solution(mesh):
    fine = Mesh(mesh.devices.reshape(16, 4, 2), ("dp", "x", "zh"))
    spec = P(None, ("x", "zh"), "dp", None)
    return jax.shard_map(
        on_device, mesh=fine, in_specs=(spec, spec, spec, P()), out_specs=spec, check_vma=False
    )
```

time: 161 us -> 145 us (0.901)
  local copies, waits for them, and re-layouts: 22.5 us -> 1.02 us
  Pallas kernels: 18.7 us -> 32.6 us
  blocking collectives: 49.9 us -> 44 us
  other arithmetic: 7.17 us -> 4.25 us
  starting transfers between devices: 21.5 us -> 24.1 us
    pallas_call x1 -> x5, Pallas kernels: 18.7 us -> 32.6 us  [the longest x1 23.3 us: attend(): pl.pallas_call(attend_kernel, in_specs=[SMEM] * 3 + [VMEM] + [HBM] * 7, o...]
    reshape x2 -> x0, local copies, waits for them, and re-layouts: 7.24 us -> none  [the longest x1 3.98 us: on_device(): return back.reshape(queries.shape)]
    another operation x3 -> x0, local copies, waits for them, and re-layouts: 6.95 us -> none  [halved(): return value.reshape(groups, rows, 2, width // 2).transpose(2, 0, 1, 3)]
    all_to_all x1, blocking collectives: 49.9 us -> 44 us  [exchange(): lax.all_to_all(value, ('zh', 'dp'), split_axis=0, concat_axis=0, tiled=True)]
    all_to_all x2, waiting for transfers between devices: 22.8 us -> 18.5 us  [exchange(): lax.all_to_all(value, ('zh', 'dp'), split_axis=0, concat_axis=0, tiled=True)]
    mul x0 -> x3, other arithmetic: none -> 3.58 us  [the longest x2 3.58 us: tables(): jnp.sin(angles) * jnp.where(lane < HALF, -1.0, 1.0)]
    neg x1 -> x0, other arithmetic: 3.49 us -> none  [on_device(): sine = jnp.concatenate([-sine, sine], -1)]
    concatenate x3 -> x0, other arithmetic: 3.46 us -> none  [the longest x1 1.28 us: on_device(): cosine = jnp.concatenate([cosine, cosine], -1)]
  transfers between devices with their start and end apart: 4 -> 6, of which waited for: 3 -> 4; matrix products, arithmetic and copies ran while one was open for 10% -> 3% of each run, Pallas kernels for 0% -> 4%
where the time goes in v2:
time: 145 us
  blocking collectives  44 us (30%)
  waiting for transfers between devices  38.9 us (27%)
  Pallas kernels  32.6 us (22%)
  starting transfers between devices  24.1 us (17%)
  other arithmetic  4.25 us (3%)
    all_to_all x1, blocking collectives, exchange(): lax.all_to_all(value, ('zh', 'dp'), split_axis=0, concat_axis=0, tiled=True)  44 us
    pallas_call x1, Pallas kernels, attend(): pl.pallas_call(attend_kernel, in_specs=[SMEM] * 3 + [VMEM] + [HBM] * 7, o...  23.3 us
    ppermute x4, waiting for transfers between devices, moved(): return lax.ppermute(value, ('dp', 'x', 'zh'), pairs)  20.4 us
    all_to_all x2, waiting for transfers between devices, exchange(): lax.all_to_all(value, ('zh', 'dp'), split_axis=0, concat_axis=0, tiled=True)  18.5 us
    all_to_all x2, starting transfers between devices, exchange(): lax.all_to_all(value, ('zh', 'dp'), split_axis=0, concat_axis=0, tiled=True)  14.6 us
    ppermute x4, starting transfers between devices, moved(): return lax.ppermute(value, ('dp', 'x', 'zh'), pairs)  9.51 us
    pallas_call x1, Pallas kernels, split_queries(): pl.pallas_call(split_queries_kernel, in_specs=[HBM, VMEM, VMEM], out_spec...  4.08 us
    mul x2, other arithmetic, tables(): jnp.sin(angles) * jnp.where(lane < HALF, -1.0, 1.0)  3.58 us
  transfers between devices with their start and end apart: 6, of which 4 were waited for; matrix products, arithmetic and copies ran while one was open for 3% of the time, Pallas kernels for 4%

profile of v2, /device:TPU:1, one launch (start us, length us, event | category | flops | bytes accessed | tf_op | source)
XLA Modules:
  0.0 145.2 jit_solution(10402166483753607710)
XLA Ops:
  0.0 2.0 %split_keys.1 = bf16[4,16,2,24,128]{4,3,2,1,0:T(8,128)(2,1)} custom-call(bf16[16,24,512]{2,1,0:T(8,128)(2,1)} %bitcast.20, bf16[16,24,512]{2,1,0:T(8,128)(2,1)} %bitcast.21), custom_call_target="tpu_custom_call" | custom-call | tf_op jit(solution)/shard_map/split_keys/pallas_call | solution.py:83
  2.0 9.6 %all-to-all-start.1 = ((bf16[32,2,2,24,128]{4,3,2,1,0:T(8,128)(2,1)}), bf16[32,2,2,24,128]{4,3,2,1,0:T(8,128)(2,1)S(1)}, u32[]{:S(2)}, u32[]{:S(2)}) async-start(bf16[32,2,2,24,128]{4,3,2,1,0:T(8,128)(2,1)} %bitcast.19), calls=%async_computation.1 | async-start | bytes 1572864 | tf_op jit(solution)/shard_map/all_to_all | solution.py:353
  11.7 0.1 add_convert_fusion
  11.8 0.8 fusion.1
  12.5 4.1 %split_queries.1 = bf16[4,16,8,24,128]{4,3,2,1,0:T(8,128)(2,1)} custom-call(bf16[16,24,4096]{2,1,0:T(8,128)(2,1)} %bitcast.18, f32[16,24,128]{2,1,0:T(8,128)S(1)} %get-tuple-element.16.cos_ref, f32[16,24,128]{2,1,0:T(8,128)S(1)} %get-tuple-element.15.sin_ref), custom_call_target="tpu_custom_call" | custom-call | flops 10000000 | bytes 6500000 | tf_op jit(solution)/shard_map/split_queries/pallas_call | solution.py:127
  16.6 9.3 %all-to-all-done.1.in_ref = bf16[32,2,2,24,128]{4,3,2,1,0:T(8,128)(2,1)S(1)} async-done(((bf16[32,2,2,24,128]{4,3,2,1,0:T(8,128)(2,1)}), bf16[32,2,2,24,128]{4,3,2,1,0:T(8,128)(2,1)S(1)}, u32[]{:S(2)}, u32[]{:S(2)}) %all-to-all-start.1) | async-done | bytes 786464 | tf_op jit(solution)/shard_map/all_to_all | solution.py:353
  25.9 0.0 copy-start.2
  25.9 0.0 copy-start.7
  25.9 0.9 copy-done.2
  26.8 5.0 %all-to-all-start = ((bf16[32,2,8,24,128]{4,3,2,1,0:T(8,128)(2,1)}), bf16[32,2,8,24,128]{4,3,2,1,0:T(8,128)(2,1)}, u32[]{:S(2)}, u32[]{:S(2)}) async-start(bf16[32,2,8,24,128]{4,3,2,1,0:T(8,128)(2,1)} %bitcast.17), calls=%async_computation | async-start | bytes 6291456 | tf_op jit(solution)/shard_map/all_to_all | solution.py:353
  31.8 0.0 copy-done.7
  31.8 0.1 select_reduce_fusion
  31.9 0.1 broadcast_add_fusion
  32.0 0.1 add_convert_fusion.1
  32.1 2.8 %fusion = (f32[2,768,128]{2,1,0:T(8,128)S(1)}, f32[2,768,128]{2,1,0:T(8,128)S(1)}) fusion(f32[128]{0:T(128)S(1)} %get-tuple-element.19, f32[128]{0:T(128)S(1)} %get-tuple-element.20, f32[2,768]{1,0:T(2,128)S(1)} %add_convert_fusion.1), kind=kLoop, calls=%fused_computation.2 | loop fusion | flops 393216 | bytes 1580032 | tf_op jit(solution)/shard_map/mul | solution.py:375
  34.9 1.4 turn_keys.1
  36.3 0.0 copy-start
  36.3 0.0 copy-start.1
  36.3 1.3 collective-permute-start
  37.6 3.1 %collective-permute-start.1 = (bf16[768,256]{1,0:T(8,128)(2,1)S(1)}, bf16[768,256]{1,0:T(8,128)(2,1)S(1)}, u32[]{:S(2)}, u32[]{:S(2)}) collective-permute-start(bf16[768,256]{1,0:T(8,128)(2,1)S(1)} %get-tuple-element.10.own1), channel_id=1, source_target_pairs={{0,2},{1,3},{2,4},{3,5},{4,6},{5,7},{6,8},{7,9},{8,10},{9,11},{10,... | collective-permute-start | bytes 1179656 | tf_op jit(solution)/shard_map/ppermute | solution.py:367
  40.7 0.2 select_reduce_fusion.1
  40.9 1.5 %collective-permute-start.2 = (bf16[384,256]{1,0:T(8,128)(2,1)S(1)}, bf16[384,256]{1,0:T(8,128)(2,1)S(1)}, u32[]{:S(2)}, u32[]{:S(2)}) collective-permute-start(bf16[384,256]{1,0:T(8,128)(2,1)S(1)} %get-tuple-element.11), channel_id=1, source_target_pairs={{0,4},{1,5},{2,6},{3,7},{4,0},{5,1},{6,2},{7,3},{8,12},{9,13},{10,... | collective-permute-start | bytes 589832 | tf_op jit(solution)/shard_map/ppermute | solution.py:367
  42.4 3.6 %collective-permute-start.3 = (bf16[384,256]{1,0:T(8,128)(2,1)S(1)}, bf16[384,256]{1,0:T(8,128)(2,1)S(1)}, u32[]{:S(2)}, u32[]{:S(2)}) collective-permute-start(bf16[384,256]{1,0:T(8,128)(2,1)S(1)} %get-tuple-element.12), channel_id=1, source_target_pairs={{0,4},{1,5},{2,6},{3,7},{4,8},{5,9},{6,10},{7,11},{8,12},{9,13},{1... | collective-permute-start | bytes 589832 | tf_op jit(solution)/shard_map/ppermute | solution.py:367
  46.0 0.1 broadcast_subtract_fusion
  46.1 0.1 sub.22.first_ref
  46.2 0.1 add_convert_fusion.2.flag_ref
  46.3 15.2 %collective-permute-done.2.far0 = bf16[384,256]{1,0:T(8,128)(2,1)S(1)} collective-permute-done((bf16[384,256]{1,0:T(8,128)(2,1)S(1)}, bf16[384,256]{1,0:T(8,128)(2,1)S(1)}, u32[]{:S(2)}, u32[]{:S(2)}) %collective-permute-start.2) | collective-permute-done | bytes 196640 | tf_op jit(solution)/shard_map/ppermute | solution.py:367
  61.5 0.0 copy-start.5
  61.5 5.2 %collective-permute-done.3.far1 = bf16[384,256]{1,0:T(8,128)(2,1)S(1)} collective-permute-done((bf16[384,256]{1,0:T(8,128)(2,1)S(1)}, bf16[384,256]{1,0:T(8,128)(2,1)S(1)}, u32[]{:S(2)}, u32[]{:S(2)}) %collective-permute-start.3) | collective-permute-done | bytes 196640 | tf_op jit(solution)/shard_map/ppermute | solution.py:367
  66.7 0.0 copy-start.6
  66.7 0.0 collective-permute-done.near0
  66.7 0.0 copy-start.3
  66.7 0.0 collective-permute-done.1.near1
  66.7 0.0 copy-start.4
  66.7 9.2 %all-to-all-done = bf16[32,2,8,24,128]{4,3,2,1,0:T(8,128)(2,1)} async-done(((bf16[32,2,8,24,128]{4,3,2,1,0:T(8,128)(2,1)}), bf16[32,2,8,24,128]{4,3,2,1,0:T(8,128)(2,1)}, u32[]{:S(2)}, u32[]{:S(2)}) %all-to-all-start) | async-done | bytes 3145760 | tf_op jit(solution)/shard_map/all_to_all | solution.py:353
  75.9 0.0 copy-done
  75.9 0.0 copy-done.1
  75.9 0.0 copy-done.5
  75.9 0.0 copy-done.6
  75.9 0.0 copy-done.3
  75.9 0.0 copy-done.4
  75.9 23.3 %attend.1 = bf16[32,2,192,128]{3,2,1,0:T(8,128)(2,1)S(1)} custom-call(s32[16]{0:T(128)S(1)} %sub.22.first_ref, s32[2]{0:T(128)S(1)} %get-tuple-element.13.base_ref, s32[2]{0:T(128)S(1)} %add_convert_fusion.2.flag_ref, s32[1,128]{1,0:T(1,128)S(1)} %bitcast.16, bf16[32,2,192,128]{3,2,1,0:T(8,128)(2,1)} %bitcast.5.q_ref, bf16[768,256]{1,0:T(8,128)(2,1)} %copy-done, ...), custom_call_target="tpu_custom_call" | custom-call | flops 8000000000 | bytes 10000000 | tf_op jit(solution)/shard_map/attend/pallas_call | solution.py:328
  99.2 44.0 %all_to_all.15 = bf16[32,2,8,24,128]{4,3,2,1,0:T(8,128)(2,1)S(1)} all-to-all(bf16[32,2,8,24,128]{4,3,2,1,0:T(8,128)(2,1)S(1)} %bitcast.15), channel_id=1, replica_groups=mesh['dp'=16,'x'=4,'zh'=2] {'zh','dp'}, dimensions={0} | all-to-all | bytes 6291456 | tf_op jit(solution)/shard_map/all_to_all | solution.py:353
  143.2 1.8 %join_heads.1 = bf16[16,24,4096]{2,1,0:T(8,128)(2,1)} custom-call(bf16[4,16,8,24,128]{4,3,2,1,0:T(8,128)(2,1)S(1)} %bitcast.14), custom_call_target="tpu_custom_call" | custom-call | tf_op jit(solution)/shard_map/join_heads/pallas_call | solution.py:167
  (5 shorter events, 0.0 us)
Async XLA Ops:
  2.0 23.8 %all-to-all-start.1 = ((bf16[32,2,2,24,128]{4,3,2,1,0:T(8,128)(2,1)}), bf16[32,2,2,24,128]{4,3,2,1,0:T(8,128)(2,1)S(1)}, u32[]{:S(2)}, u32[]{:S(2)}) async-start(bf16[32,2,2,24,128]{4,3,2,1,0:T(8,128)(2,1)} %bitcast.19), calls=%async_computation.1 | async-start | bytes 1572864 | tf_op jit(solution)/shard_map/all_to_all | solution.py:353
  25.9 0.9 copy-start.2
  25.9 5.9 %copy-start.7 = (s32[64]{0:T(128)S(1)}, s32[64]{0:T(128)}, u32[]{:S(2)}) copy-start(s32[64]{0:T(128)} %param.7) | copy-start | bytes 772
  26.8 49.1 %all-to-all-start = ((bf16[32,2,8,24,128]{4,3,2,1,0:T(8,128)(2,1)}), bf16[32,2,8,24,128]{4,3,2,1,0:T(8,128)(2,1)}, u32[]{:S(2)}, u32[]{:S(2)}) async-start(bf16[32,2,8,24,128]{4,3,2,1,0:T(8,128)(2,1)} %bitcast.17), calls=%async_computation | async-start | bytes 6291456 | tf_op jit(solution)/shard_map/all_to_all | solution.py:353
  36.3 39.6 %copy-start = (bf16[768,256]{1,0:T(8,128)(2,1)}, bf16[768,256]{1,0:T(8,128)(2,1)S(1)}, u32[]{:S(2)}) copy-start(bf16[768,256]{1,0:T(8,128)(2,1)S(1)} %get-tuple-element.9.own0) | copy-start | bytes 1179652
  36.3 39.6 %copy-start.1 = (bf16[768,256]{1,0:T(8,128)(2,1)}, bf16[768,256]{1,0:T(8,128)(2,1)S(1)}, u32[]{:S(2)}) copy-start(bf16[768,256]{1,0:T(8,128)(2,1)S(1)} %get-tuple-element.10.own1) | copy-start | bytes 1179652
  36.3 30.4 %collective-permute-start = (bf16[768,256]{1,0:T(8,128)(2,1)S(1)}, bf16[768,256]{1,0:T(8,128)(2,1)S(1)}, u32[]{:S(2)}, u32[]{:S(2)}) collective-permute-start(bf16[768,256]{1,0:T(8,128)(2,1)S(1)} %get-tuple-element.9.own0), channel_id=1, source_target_pairs={{0,2},{1,3},{2,4},{3,5},{4,6},{5,7},{6,0},{7,1},{8,10},{9,11},{10,... | collective-permute-start | bytes 1179656 | tf_op jit(solution)/shard_map/ppermute | solution.py:367
  37.6 29.1 %collective-permute-start.1 = (bf16[768,256]{1,0:T(8,128)(2,1)S(1)}, bf16[768,256]{1,0:T(8,128)(2,1)S(1)}, u32[]{:S(2)}, u32[]{:S(2)}) collective-permute-start(bf16[768,256]{1,0:T(8,128)(2,1)S(1)} %get-tuple-element.10.own1), channel_id=1, source_target_pairs={{0,2},{1,3},{2,4},{3,5},{4,6},{5,7},{6,8},{7,9},{8,10},{9,11},{10,... | collective-permute-start | bytes 1179656 | tf_op jit(solution)/shard_map/ppermute | solution.py:367
  40.9 20.6 %collective-permute-start.2 = (bf16[384,256]{1,0:T(8,128)(2,1)S(1)}, bf16[384,256]{1,0:T(8,128)(2,1)S(1)}, u32[]{:S(2)}, u32[]{:S(2)}) collective-permute-start(bf16[384,256]{1,0:T(8,128)(2,1)S(1)} %get-tuple-element.11), channel_id=1, source_target_pairs={{0,4},{1,5},{2,6},{3,7},{4,0},{5,1},{6,2},{7,3},{8,12},{9,13},{10,... | collective-permute-start | bytes 589832 | tf_op jit(solution)/shard_map/ppermute | solution.py:367
  42.4 24.3 %collective-permute-start.3 = (bf16[384,256]{1,0:T(8,128)(2,1)S(1)}, bf16[384,256]{1,0:T(8,128)(2,1)S(1)}, u32[]{:S(2)}, u32[]{:S(2)}) collective-permute-start(bf16[384,256]{1,0:T(8,128)(2,1)S(1)} %get-tuple-element.12), channel_id=1, source_target_pairs={{0,4},{1,5},{2,6},{3,7},{4,8},{5,9},{6,10},{7,11},{8,12},{9,13},{1... | collective-permute-start | bytes 589832 | tf_op jit(solution)/shard_map/ppermute | solution.py:367
  61.5 14.4 %copy-start.5 = (bf16[384,256]{1,0:T(8,128)(2,1)}, bf16[384,256]{1,0:T(8,128)(2,1)S(1)}, u32[]{:S(2)}) copy-start(bf16[384,256]{1,0:T(8,128)(2,1)S(1)} %collective-permute-done.2.far0) | copy-start | bytes 589828
  66.7 9.3 %copy-start.6 = (bf16[384,256]{1,0:T(8,128)(2,1)}, bf16[384,256]{1,0:T(8,128)(2,1)S(1)}, u32[]{:S(2)}) copy-start(bf16[384,256]{1,0:T(8,128)(2,1)S(1)} %collective-permute-done.3.far1) | copy-start | bytes 589828
  66.7 9.3 %copy-start.3 = (bf16[768,256]{1,0:T(8,128)(2,1)}, bf16[768,256]{1,0:T(8,128)(2,1)S(1)}, u32[]{:S(2)}) copy-start(bf16[768,256]{1,0:T(8,128)(2,1)S(1)} %collective-permute-done.near0) | copy-start | bytes 1179652
  66.7 9.3 %copy-start.4 = (bf16[768,256]{1,0:T(8,128)(2,1)}, bf16[768,256]{1,0:T(8,128)(2,1)S(1)}, u32[]{:S(2)}) copy-start(bf16[768,256]{1,0:T(8,128)(2,1)S(1)} %collective-permute-done.1.near1) | copy-start | bytes 1179652

commit v3 on v2

--- a/solution.py
+++ b/solution.py
@@ -20,15 +20,17 @@
 PER_KV = QUERY_HEADS // KEY_VALUE_HEADS
 PEERS = 32
 PIECE = PER_KV * ROWS
-TILE = 96
+TILE = 48
 SOURCES = TILE // ROWS
 WINDOW = 256
 STEPS = PAIR // TILE
+UNITS = SLOTS * STEPS
+TEAM = 4
 MOST = 5
 REACH = MOST * WINDOW
 PAD = REACH - HALO - TILE
 KEYS = PAD + HALO + PAIR
-PARTS = 2
+SIZE = SOURCES * PIECE
 SCALE = 1.4426950408889634 / WIDTH**0.5
 LOW = -1e30
 MIB = 1024 * 1024
@@ -198,14 +200,13 @@
         out_shape=[jax.ShapeDtypeStruct((PAIR, 2 * WIDTH), jnp.bfloat16)] * 2
         + [jax.ShapeDtypeStruct((FAR, 2 * WIDTH), jnp.bfloat16)] * 2,
         **small(12, name="turn_keys"),
-    )(stored(own), cosine, sine)
+    )(own, cosine, sine)
 
 
 def attend_kernel(
-    first_ref, base_ref, flag_ref, ends_ref, q_ref, own0, own1, near0, near1, far0, far1, out_ref,
-    q_held, k_ref, v_ref, start_ref, bias_ref, s_ref, p_ref, q_sems, k_sems, v_sems,
+    order_ref, most_ref, base_ref, flag_ref, ends_ref, q_ref, own0, own1, near0, near1, far0, far1,
+    out_ref, q_held, k_ref, v_ref, start_ref, bias_ref, s_ref, p_ref, q_sems, k_sems, v_sems,
 ):
-    size = PARTS * PIECE
     pieces = []
     for place, (pair, base, flag) in enumerate((
         ((own0, own1), PAD + HALO, 0),
@@ -232,12 +233,12 @@
             q_ref.at[pl.ds(step * SOURCES, SOURCES), slot], q_held.at[index], q_sems.at[index]
         )
 
-    for index in range(SLOTS * STEPS):
-        arrival(index).start()
+    for index in range(UNITS):
+        arrival(order_ref[index]).start()
     for slot in range(SLOTS):
         k_ref[slot, :PAD, :] = jnp.zeros((PAD, WIDTH), jnp.bfloat16)
         v_ref[slot, :PAD, :] = jnp.zeros((PAD, WIDTH), jnp.bfloat16)
-    for index in range(SLOTS * STEPS):
+    for index in range(UNITS):
         base = base_ref[index // STEPS]
         ends = jnp.broadcast_to(ends_ref[...] - base, (TILE, WIDTH))
         own = PAD + HALO + index % STEPS * TILE
@@ -247,106 +248,103 @@
     for copy in pieces:
         copy.wait()
 
-    def one_step(index, _):
-        slot, step = index // STEPS, index % STEPS
-        stop = step * TILE + REACH
-        windows = (stop - first_ref[index] + WINDOW - 1) // WINDOW
-        arrival(index).wait()
+    def one_team(team, _):
+        units = [order_ref[team * TEAM + i] for i in range(TEAM)]
+        slots = [unit // STEPS for unit in units]
+        steps = [unit % STEPS for unit in units]
+        stops = [step * TILE + REACH for step in steps]
+        for unit in units:
+            arrival(unit).wait()
 
         for count in range(1, MOST + 1):
 
-            @pl.when(windows == count)
+            @pl.when(most_ref[team] == count)
             def _():
                 width = count * WINDOW
-                begin = pl.multiple_of(stop - width, 32)
-                lane = lax.broadcasted_iota(jnp.int32, (TILE, WIDTH), 1)
-                row = stop - TILE + lax.broadcasted_iota(jnp.int32, (TILE, WIDTH), 0)
-                start = start_ref[index]
-                for column in range(0, width, WIDTH):
-                    key = lane + (begin + column)
-                    allowed = (key >= start) & (key <= row)
-                    bias_ref[:, pl.ds(column, WIDTH)] = jnp.where(allowed, 0.0, LOW)
-
-                def score(turn):
-                    q = q_held[index, pl.ds(turn * PARTS, PARTS)].reshape(size, WIDTH)
-                    rows = pl.ds(turn * PARTS * ROWS, PARTS * ROWS)
+                begins = [pl.multiple_of(stop - width, 16) for stop in stops]
+
+                def score(i):
+                    lane = lax.broadcasted_iota(jnp.int32, (TILE, WIDTH), 1) + begins[i]
+                    row = stops[i] - TILE + lax.broadcasted_iota(jnp.int32, (TILE, WIDTH), 0)
+                    start = start_ref[units[i]]
+                    for column in range(0, width, WIDTH):
+                        key = lane + column
+                        allowed = (key >= start) & (key <= row)
+                        bias_ref[i, :, pl.ds(column, WIDTH)] = jnp.where(allowed, 0.0, LOW)
+                    q = q_held[units[i]].reshape(SIZE, WIDTH)
                     top = None
                     for window in range(count):
-                        here = pl.ds(pl.multiple_of(begin + window * WINDOW, 32), WINDOW)
+                        here = pl.ds(pl.multiple_of(begins[i] + window * WINDOW, 16), WINDOW)
                         scores = lax.dot_general(
                             q,
-                            k_ref[slot, here, :],
+                            k_ref[slots[i], here, :],
                             (((1,), (1,)), ((), ())),
                             preferred_element_type=jnp.float32,
                         )
-                        bias = bias_ref[rows, pl.ds(window * WINDOW, WINDOW)]
-                        scores = scores.reshape(PARTS, PER_KV, ROWS, WINDOW)
-                        scores = scores + bias.reshape(PARTS, 1, ROWS, WINDOW)
-                        scores = scores.reshape(size, WINDOW)
-                        s_ref[turn, :, pl.ds(window * WINDOW, WINDOW)] = scores
+                        bias = bias_ref[i, :, pl.ds(window * WINDOW, WINDOW)]
+                        scores = scores.reshape(SOURCES, PER_KV, ROWS, WINDOW)
+                        scores = scores + bias.reshape(SOURCES, 1, ROWS, WINDOW)
+                        scores = scores.reshape(SIZE, WINDOW)
+                        s_ref[i, :, pl.ds(window * WINDOW, WINDOW)] = scores
                         high = jnp.maximum(scores[:, :WIDTH], scores[:, WIDTH:])
                         top = high if top is None else jnp.maximum(top, high)
                     return jnp.max(top, axis=1, keepdims=True)
 
-                def weigh(turn, top):
+                def weigh(i, top):
                     total = None
                     for window in range(count):
                         here = pl.ds(window * WINDOW, WINDOW)
-                        weights = jnp.exp2((s_ref[turn, :, here] - top) * SCALE)
-                        p_ref[turn, :, here] = weights.astype(jnp.bfloat16)
+                        weights = jnp.exp2((s_ref[i, :, here] - top) * SCALE)
+                        p_ref[i, :, here] = weights.astype(jnp.bfloat16)
                         both = weights[:, :WIDTH] + weights[:, WIDTH:]
                         total = both if total is None else total + both
                     return jnp.sum(total, axis=1, keepdims=True)
 
-                def mix(turn, total):
+                def mix(i, total):
                     mixed = jnp.dot(
-                        p_ref[turn, :, :width],
-                        v_ref[slot, pl.ds(begin, width), :],
+                        p_ref[i, :, :width],
+                        v_ref[slots[i], pl.ds(begins[i], width), :],
                         preferred_element_type=jnp.float32,
                     )
                     result = (mixed / total).astype(jnp.bfloat16)
-                    for part in range(PARTS):
-                        out_ref[step * SOURCES + turn * PARTS + part, slot] = result[
-                            part * PIECE : (part + 1) * PIECE
-                        ]
-
-                turns = SOURCES // PARTS
+                    out_ref[pl.ds(steps[i] * SOURCES, SOURCES), slots[i]] = result.reshape(
+                        SOURCES, PIECE, WIDTH
+                    )
+
                 tops = [score(0)]
-                for turn in range(turns):
-                    if turn + 1 < turns:
-                        tops.append(score(turn + 1))
-                    mix(turn, weigh(turn, tops[turn]))
+                for i in range(TEAM):
+                    if i + 1 < TEAM:
+                        tops.append(score(i + 1))
+                    mix(i, weigh(i, tops[i]))
 
         return 0
 
-    lax.fori_loop(0, SLOTS * STEPS, one_step, 0)
-
-
-def attend(first, base, flags, ends, q, own, near, far):
-    size = PARTS * PIECE
-    turns = SOURCES // PARTS
+    lax.fori_loop(0, UNITS // TEAM, one_team, 0)
+
+
+def attend(order, most, base, flags, ends, q, own, near, far):
     return pl.pallas_call(
         attend_kernel,
-        in_specs=[SMEM] * 3 + [VMEM] + [HBM] * 7,
+        in_specs=[SMEM] * 4 + [VMEM] + [HBM] * 7,
         out_specs=VMEM,
         out_shape=pltpu.VMEM((PEERS, SLOTS, PIECE, WIDTH), jnp.bfloat16),
         scratch_shapes=[
-            pltpu.VMEM((SLOTS * STEPS, SOURCES, PIECE, WIDTH), jnp.bfloat16),
+            pltpu.VMEM((UNITS, SOURCES, PIECE, WIDTH), jnp.bfloat16),
             pltpu.VMEM((SLOTS, KEYS, WIDTH), jnp.bfloat16),
             pltpu.VMEM((SLOTS, KEYS, WIDTH), jnp.bfloat16),
-            pltpu.VMEM((SLOTS * STEPS, TILE, WIDTH), jnp.int32),
-            pltpu.VMEM((TILE, REACH), jnp.float32),
-            pltpu.VMEM((turns, size, REACH), jnp.float32),
-            pltpu.VMEM((turns, size, REACH), jnp.bfloat16),
-            pltpu.SemaphoreType.DMA((SLOTS * STEPS,)),
+            pltpu.VMEM((UNITS, TILE, WIDTH), jnp.int32),
+            pltpu.VMEM((TEAM, TILE, REACH), jnp.float32),
+            pltpu.VMEM((TEAM, SIZE, REACH), jnp.float32),
+            pltpu.VMEM((TEAM, SIZE, REACH), jnp.bfloat16),
+            pltpu.SemaphoreType.DMA((UNITS,)),
             pltpu.SemaphoreType.DMA((3 * SLOTS,)),
             pltpu.SemaphoreType.DMA((3 * SLOTS,)),
         ],
         cost_estimate=pl.CostEstimate(
             flops=8_000_000_000, bytes_accessed=10_000_000, transcendentals=12_000_000
         ),
-        **small(24, name="attend"),
-    )(first, base, flags, ends, *map(stored, (q,) + own + near + far))
+        **small(32, name="attend"),
+    )(order, most, base, flags, ends, *map(stored, (q,) + own + near + far))
 
 
 def exchange(value):
@@ -386,12 +384,13 @@
         + dp * ROWS
         + jnp.arange(ROWS, dtype=jnp.int32)[None, :]
     )
-    q = split_queries(queries.reshape(GROUPS, ROWS, -1), *tables(home))
-    q = exchange(q.reshape(PEERS, SLOTS, PER_KV, ROWS, WIDTH))
-
     base = (dp % 8 * SLOTS + jnp.arange(SLOTS, dtype=jnp.int32)) * GROUP + x * PAIR
     positions = base[:, None] + jnp.arange(PAIR, dtype=jnp.int32)[None, :]
-    own0, own1, last0, last1 = turn_keys(own, *tables(positions))
+    turns = lax.optimization_barrier((*tables(home), *tables(positions)))
+    q = split_queries(queries.reshape(GROUPS, ROWS, -1), *turns[:2])
+    q = exchange(q.reshape(PEERS, SLOTS, PER_KV, ROWS, WIDTH))
+
+    own0, own1, last0, last1 = turn_keys(own, *turns[2:])
     near = moved(own0, 0, 1), moved(own1, 1, 1)
     far = moved(last0, 0, 2), moved(last1, 1, 2)
     flags = jnp.stack([(x < 2).astype(jnp.int32), (x < 1).astype(jnp.int32)])
@@ -401,10 +400,19 @@
     ends = jnp.sum(jnp.where(docs[:, None] <= docs[None, :], lengths[:, None], 0), axis=0)
     heads = base[:, None] + jnp.arange(0, PAIR, TILE, dtype=jnp.int32)[None, :]
     first = jnp.max(jnp.where(ends <= heads[..., None], ends, 0), axis=-1)
+    need = (heads + TILE - first + WINDOW - 1) // WINDOW
+    need, unit = need.reshape(-1), jnp.arange(UNITS, dtype=jnp.int32)
+    earlier = (need[None, :] > need[:, None]) | (
+        (need[None, :] == need[:, None]) & (unit[None, :] < unit[:, None])
+    )
+    rank = jnp.sum(earlier.astype(jnp.int32), axis=1)
+    order = jnp.sum(jnp.where(rank[None, :] == unit[:, None], unit[None, :], 0), axis=1)
+    most = jnp.sum(jnp.where(rank[None, :] == unit[::TEAM, None], need[None, :], 0), axis=1)
     base = base - PAD - HALO
 
     mixed = attend(
-        (first - base[:, None]).reshape(-1),
+        order,
+        most,
         base,
         flags,
         ends[None, :],

time: 145 us -> 142 us (0.979)
  Pallas kernels: 32.6 us -> 27.4 us
    pallas_call x1, Pallas kernels: 23.3 us -> 19.2 us  [attend(): pl.pallas_call(attend_kernel, in_specs=[SMEM] * 4 + [VMEM] + [HBM] * 7, o...]
  transfers between devices with their start and end apart: 6 -> 6, of which waited for: 4 -> 4; matrix products, arithmetic and copies ran while one was open for 3% -> 3% of each run, Pallas kernels for 4% -> 3%
where the time goes in v3:
time: 142 us; the launch traced here: 141 us
  blocking collectives  44.9 us (32%)
  waiting for transfers between devices  39.3 us (28%)
  Pallas kernels  27.4 us (19%)
  starting transfers between devices  24.2 us (17%)
  other arithmetic  4.74 us (3%)
    all_to_all x1, blocking collectives, exchange(): lax.all_to_all(value, ('zh', 'dp'), split_axis=0, concat_axis=0, tiled=True)  44.9 us
    ppermute x4, waiting for transfers between devices, moved(): return lax.ppermute(value, ('dp', 'x', 'zh'), pairs)  20.2 us
    pallas_call x1, Pallas kernels, attend(): pl.pallas_call(attend_kernel, in_specs=[SMEM] * 4 + [VMEM] + [HBM] * 7, o...  19.2 us
    all_to_all x2, waiting for transfers between devices, exchange(): lax.all_to_all(value, ('zh', 'dp'), split_axis=0, concat_axis=0, tiled=True)  19.2 us
    all_to_all x2, starting transfers between devices, exchange(): lax.all_to_all(value, ('zh', 'dp'), split_axis=0, concat_axis=0, tiled=True)  14.7 us
    ppermute x4, starting transfers between devices, moved(): return lax.ppermute(value, ('dp', 'x', 'zh'), pairs)  9.51 us
    pallas_call x1, Pallas kernels, split_queries(): pl.pallas_call(split_queries_kernel, in_specs=[HBM, VMEM, VMEM], out_spec...  4.08 us
    mul x2, other arithmetic, tables(): jnp.sin(angles) * jnp.where(lane < HALF, -1.0, 1.0)  3.58 us
  transfers between devices with their start and end apart: 6, of which 4 were waited for; matrix products, arithmetic and copies ran while one was open for 3% of the time, Pallas kernels for 3%

profile of v3, /device:TPU:1, one launch (start us, length us, event | category | flops | bytes accessed | tf_op | source)
XLA Modules:
  0.0 141.2 jit_solution(2630369947726721386)
XLA Ops:
  0.0 2.0 %split_keys.1 = bf16[4,16,2,24,128]{4,3,2,1,0:T(8,128)(2,1)} custom-call(bf16[16,24,512]{2,1,0:T(8,128)(2,1)} %bitcast.20, bf16[16,24,512]{2,1,0:T(8,128)(2,1)} %bitcast.21), custom_call_target="tpu_custom_call" | custom-call | tf_op jit(solution)/shard_map/split_keys/pallas_call | solution.py:85
  2.0 9.6 %all-to-all-start.1 = ((bf16[32,2,2,24,128]{4,3,2,1,0:T(8,128)(2,1)}), bf16[32,2,2,24,128]{4,3,2,1,0:T(8,128)(2,1)S(1)}, u32[]{:S(2)}, u32[]{:S(2)}) async-start(bf16[32,2,2,24,128]{4,3,2,1,0:T(8,128)(2,1)} %bitcast.19), calls=%async_computation.1 | async-start | bytes 1572864 | tf_op jit(solution)/shard_map/all_to_all | solution.py:351
  11.7 0.1 add_convert_fusion.1
  11.8 0.1 add_convert_fusion
  11.8 0.8 fusion.1
  12.6 2.8 %fusion = (f32[2,768,128]{2,1,0:T(8,128)S(1)}, f32[2,768,128]{2,1,0:T(8,128)S(1)}) fusion(f32[128]{0:T(128)S(1)} %get-tuple-element.27, f32[128]{0:T(128)S(1)} %get-tuple-element.28, f32[2,768]{1,0:T(2,128)S(1)} %add_convert_fusion.1), kind=kLoop, calls=%fused_computation.2 | loop fusion | flops 393216 | bytes 1580032 | tf_op jit(solution)/shard_map/mul | solution.py:373
  15.4 4.1 %split_queries.1 = bf16[4,16,8,24,128]{4,3,2,1,0:T(8,128)(2,1)} custom-call(bf16[16,24,4096]{2,1,0:T(8,128)(2,1)} %bitcast.18, f32[16,24,128]{2,1,0:T(8,128)S(1)} %get-tuple-element.13.cos_ref, f32[16,24,128]{2,1,0:T(8,128)S(1)} %get-tuple-element.14.sin_ref), custom_call_target="tpu_custom_call" | custom-call | flops 10000000 | bytes 6500000 | tf_op jit(solution)/shard_map/split_queries/pallas_call | solution.py:129
  19.5 6.3 %all-to-all-done.1.in_ref = bf16[32,2,2,24,128]{4,3,2,1,0:T(8,128)(2,1)S(1)} async-done(((bf16[32,2,2,24,128]{4,3,2,1,0:T(8,128)(2,1)}), bf16[32,2,2,24,128]{4,3,2,1,0:T(8,128)(2,1)S(1)}, u32[]{:S(2)}, u32[]{:S(2)}) %all-to-all-start.1) | async-done | bytes 786464 | tf_op jit(solution)/shard_map/all_to_all | solution.py:351
  25.9 0.0 copy-start.6
  25.9 5.1 %all-to-all-start = ((bf16[32,2,8,24,128]{4,3,2,1,0:T(8,128)(2,1)}), bf16[32,2,8,24,128]{4,3,2,1,0:T(8,128)(2,1)}, u32[]{:S(2)}, u32[]{:S(2)}) async-start(bf16[32,2,8,24,128]{4,3,2,1,0:T(8,128)(2,1)} %bitcast.17), calls=%async_computation | async-start | bytes 6291456 | tf_op jit(solution)/shard_map/all_to_all | solution.py:351
  31.0 0.0 copy-done.6
  31.0 0.1 select_reduce_fusion
  31.1 0.1 broadcast_add_fusion
  31.2 0.2 select_reduce_fusion.2
  31.4 0.1 subtract_add_fusion
  31.4 0.1 sub.37
  31.5 0.3 turn_keys.1
  31.9 0.0 copy-start
  31.9 0.0 copy-start.1
  31.9 1.3 collective-permute-start
  33.2 3.1 %collective-permute-start.1 = (bf16[768,256]{1,0:T(8,128)(2,1)S(1)}, bf16[768,256]{1,0:T(8,128)(2,1)S(1)}, u32[]{:S(2)}, u32[]{:S(2)}) collective-permute-start(bf16[768,256]{1,0:T(8,128)(2,1)S(1)} %get-tuple-element.18.own1), channel_id=1, source_target_pairs={{0,2},{1,3},{2,4},{3,5},{4,6},{5,7},{6,8},{7,9},{8,10},{9,11},{10,... | collective-permute-start | bytes 1179656 | tf_op jit(solution)/shard_map/ppermute | solution.py:365
  36.3 0.2 convert_reduce_fusion
  36.5 0.1 slice.3
  36.6 0.1 select_reduce_fusion.1.order_ref
  36.7 1.5 %collective-permute-start.2 = (bf16[384,256]{1,0:T(8,128)(2,1)S(1)}, bf16[384,256]{1,0:T(8,128)(2,1)S(1)}, u32[]{:S(2)}, u32[]{:S(2)}) collective-permute-start(bf16[384,256]{1,0:T(8,128)(2,1)S(1)} %get-tuple-element.19), channel_id=1, source_target_pairs={{0,4},{1,5},{2,6},{3,7},{4,0},{5,1},{6,2},{7,3},{8,12},{9,13},{10,... | collective-permute-start | bytes 589832 | tf_op jit(solution)/shard_map/ppermute | solution.py:365
  38.2 3.6 %collective-permute-start.3 = (bf16[384,256]{1,0:T(8,128)(2,1)S(1)}, bf16[384,256]{1,0:T(8,128)(2,1)S(1)}, u32[]{:S(2)}, u32[]{:S(2)}) collective-permute-start(bf16[384,256]{1,0:T(8,128)(2,1)S(1)} %get-tuple-element.20), channel_id=1, source_target_pairs={{0,4},{1,5},{2,6},{3,7},{4,8},{5,9},{6,10},{7,11},{8,12},{9,13},{1... | collective-permute-start | bytes 589832 | tf_op jit(solution)/shard_map/ppermute | solution.py:365
  41.8 0.1 add_convert_fusion.2.flag_ref
  41.9 0.2 select_reduce_fusion.3.most_ref
  42.1 15.1 %collective-permute-done.2.far0 = bf16[384,256]{1,0:T(8,128)(2,1)S(1)} collective-permute-done((bf16[384,256]{1,0:T(8,128)(2,1)S(1)}, bf16[384,256]{1,0:T(8,128)(2,1)S(1)}, u32[]{:S(2)}, u32[]{:S(2)}) %collective-permute-start.2) | collective-permute-done | bytes 196640 | tf_op jit(solution)/shard_map/ppermute | solution.py:365
  57.2 0.0 copy-start.4
  57.2 5.1 %collective-permute-done.3.far1 = bf16[384,256]{1,0:T(8,128)(2,1)S(1)} collective-permute-done((bf16[384,256]{1,0:T(8,128)(2,1)S(1)}, bf16[384,256]{1,0:T(8,128)(2,1)S(1)}, u32[]{:S(2)}, u32[]{:S(2)}) %collective-permute-start.3) | collective-permute-done | bytes 196640 | tf_op jit(solution)/shard_map/ppermute | solution.py:365
  62.2 0.0 copy-start.5
  62.3 0.0 collective-permute-done.near0
  62.3 0.0 copy-start.2
  62.3 0.0 collective-permute-done.1.near1
  62.3 0.0 copy-start.3
  62.3 12.8 %all-to-all-done = bf16[32,2,8,24,128]{4,3,2,1,0:T(8,128)(2,1)} async-done(((bf16[32,2,8,24,128]{4,3,2,1,0:T(8,128)(2,1)}), bf16[32,2,8,24,128]{4,3,2,1,0:T(8,128)(2,1)}, u32[]{:S(2)}, u32[]{:S(2)}) %all-to-all-start) | async-done | bytes 3145760 | tf_op jit(solution)/shard_map/all_to_all | solution.py:351
  75.1 0.0 copy-done
  75.1 0.0 copy-done.1
  75.1 0.0 copy-done.4
  75.1 0.0 copy-done.5
  75.1 0.0 copy-done.2
  75.1 0.0 copy-done.3
  75.1 19.2 %attend.1 = bf16[32,2,192,128]{3,2,1,0:T(8,128)(2,1)S(1)} custom-call(s32[32]{0:T(128)S(1)} %select_reduce_fusion.1.order_ref, s32[8]{0:T(128)S(1)} %select_reduce_fusion.3.most_ref, s32[2]{0:T(128)S(1)} %get-tuple-element.21.base_ref, s32[2]{0:T(128)S(1)} %add_convert_fusion.2.flag_ref, s32[1,128]{1,0:T(1,128)S(1)} %bitcast.16, ...), custom_call_target="tpu_custom_call" | custom-call | flops 8000000000 | bytes 10000000 | tf_op jit(solution)/shard_map/attend/pallas_call | solution.py:326
  94.3 44.9 %all_to_all.15 = bf16[32,2,8,24,128]{4,3,2,1,0:T(8,128)(2,1)S(1)} all-to-all(bf16[32,2,8,24,128]{4,3,2,1,0:T(8,128)(2,1)S(1)} %bitcast.15), channel_id=1, replica_groups=mesh['dp'=16,'x'=4,'zh'=2] {'zh','dp'}, dimensions={0} | all-to-all | bytes 6291456 | tf_op jit(solution)/shard_map/all_to_all | solution.py:351
  139.2 1.8 %join_heads.1 = bf16[16,24,4096]{2,1,0:T(8,128)(2,1)} custom-call(bf16[4,16,8,24,128]{4,3,2,1,0:T(8,128)(2,1)S(1)} %bitcast.14), custom_call_target="tpu_custom_call" | custom-call | tf_op jit(solution)/shard_map/join_heads/pallas_call | solution.py:169
  (7 shorter events, 0.0 us)
Async XLA Ops:
  2.0 23.8 %all-to-all-start.1 = ((bf16[32,2,2,24,128]{4,3,2,1,0:T(8,128)(2,1)}), bf16[32,2,2,24,128]{4,3,2,1,0:T(8,128)(2,1)S(1)}, u32[]{:S(2)}, u32[]{:S(2)}) async-start(bf16[32,2,2,24,128]{4,3,2,1,0:T(8,128)(2,1)} %bitcast.19), calls=%async_computation.1 | async-start | bytes 1572864 | tf_op jit(solution)/shard_map/all_to_all | solution.py:351
  25.9 5.1 %copy-start.6 = (s32[64]{0:T(128)S(1)}, s32[64]{0:T(128)}, u32[]{:S(2)}) copy-start(s32[64]{0:T(128)} %param.7) | copy-start | bytes 772
  25.9 49.2 %all-to-all-start = ((bf16[32,2,8,24,128]{4,3,2,1,0:T(8,128)(2,1)}), bf16[32,2,8,24,128]{4,3,2,1,0:T(8,128)(2,1)}, u32[]{:S(2)}, u32[]{:S(2)}) async-start(bf16[32,2,8,24,128]{4,3,2,1,0:T(8,128)(2,1)} %bitcast.17), calls=%async_computation | async-start | bytes 6291456 | tf_op jit(solution)/shard_map/all_to_all | solution.py:351
  31.9 43.2 %copy-start = (bf16[768,256]{1,0:T(8,128)(2,1)}, bf16[768,256]{1,0:T(8,128)(2,1)S(1)}, u32[]{:S(2)}) copy-start(bf16[768,256]{1,0:T(8,128)(2,1)S(1)} %get-tuple-element.17.own0) | copy-start | bytes 1179652
  31.9 43.2 %copy-start.1 = (bf16[768,256]{1,0:T(8,128)(2,1)}, bf16[768,256]{1,0:T(8,128)(2,1)S(1)}, u32[]{:S(2)}) copy-start(bf16[768,256]{1,0:T(8,128)(2,1)S(1)} %get-tuple-element.18.own1) | copy-start | bytes 1179652
  31.9 30.4 %collective-permute-start = (bf16[768,256]{1,0:T(8,128)(2,1)S(1)}, bf16[768,256]{1,0:T(8,128)(2,1)S(1)}, u32[]{:S(2)}, u32[]{:S(2)}) collective-permute-start(bf16[768,256]{1,0:T(8,128)(2,1)S(1)} %get-tuple-element.17.own0), channel_id=1, source_target_pairs={{0,2},{1,3},{2,4},{3,5},{4,6},{5,7},{6,0},{7,1},{8,10},{9,11},{10,... | collective-permute-start | bytes 1179656 | tf_op jit(solution)/shard_map/ppermute | solution.py:365
  33.2 29.1 %collective-permute-start.1 = (bf16[768,256]{1,0:T(8,128)(2,1)S(1)}, bf16[768,256]{1,0:T(8,128)(2,1)S(1)}, u32[]{:S(2)}, u32[]{:S(2)}) collective-permute-start(bf16[768,256]{1,0:T(8,128)(2,1)S(1)} %get-tuple-element.18.own1), channel_id=1, source_target_pairs={{0,2},{1,3},{2,4},{3,5},{4,6},{5,7},{6,8},{7,9},{8,10},{9,11},{10,... | collective-permute-start | bytes 1179656 | tf_op jit(solution)/shard_map/ppermute | solution.py:365
  36.7 20.5 %collective-permute-start.2 = (bf16[384,256]{1,0:T(8,128)(2,1)S(1)}, bf16[384,256]{1,0:T(8,128)(2,1)S(1)}, u32[]{:S(2)}, u32[]{:S(2)}) collective-permute-start(bf16[384,256]{1,0:T(8,128)(2,1)S(1)} %get-tuple-element.19), channel_id=1, source_target_pairs={{0,4},{1,5},{2,6},{3,7},{4,0},{5,1},{6,2},{7,3},{8,12},{9,13},{10,... | collective-permute-start | bytes 589832 | tf_op jit(solution)/shard_map/ppermute | solution.py:365
  38.2 24.0 %collective-permute-start.3 = (bf16[384,256]{1,0:T(8,128)(2,1)S(1)}, bf16[384,256]{1,0:T(8,128)(2,1)S(1)}, u32[]{:S(2)}, u32[]{:S(2)}) collective-permute-start(bf16[384,256]{1,0:T(8,128)(2,1)S(1)} %get-tuple-element.20), channel_id=1, source_target_pairs={{0,4},{1,5},{2,6},{3,7},{4,8},{5,9},{6,10},{7,11},{8,12},{9,13},{1... | collective-permute-start | bytes 589832 | tf_op jit(solution)/shard_map/ppermute | solution.py:365
  57.2 17.9 %copy-start.4 = (bf16[384,256]{1,0:T(8,128)(2,1)}, bf16[384,256]{1,0:T(8,128)(2,1)S(1)}, u32[]{:S(2)}) copy-start(bf16[384,256]{1,0:T(8,128)(2,1)S(1)} %collective-permute-done.2.far0) | copy-start | bytes 589828
  62.2 12.9 %copy-start.5 = (bf16[384,256]{1,0:T(8,128)(2,1)}, bf16[384,256]{1,0:T(8,128)(2,1)S(1)}, u32[]{:S(2)}) copy-start(bf16[384,256]{1,0:T(8,128)(2,1)S(1)} %collective-permute-done.3.far1) | copy-start | bytes 589828
  62.3 12.9 %copy-start.2 = (bf16[768,256]{1,0:T(8,128)(2,1)}, bf16[768,256]{1,0:T(8,128)(2,1)S(1)}, u32[]{:S(2)}) copy-start(bf16[768,256]{1,0:T(8,128)(2,1)S(1)} %collective-permute-done.near0) | copy-start | bytes 1179652
  62.3 12.9 %copy-start.3 = (bf16[768,256]{1,0:T(8,128)(2,1)}, bf16[768,256]{1,0:T(8,128)(2,1)S(1)}, u32[]{:S(2)}) copy-start(bf16[768,256]{1,0:T(8,128)(2,1)S(1)} %collective-permute-done.1.near1) | copy-start | bytes 1179652

commit v4 on v3

--- a/solution.py
+++ b/solution.py
@@ -288,7 +288,8 @@
                         s_ref[i, :, pl.ds(window * WINDOW, WINDOW)] = scores
                         high = jnp.maximum(scores[:, :WIDTH], scores[:, WIDTH:])
                         top = high if top is None else jnp.maximum(top, high)
-                    return jnp.max(top, axis=1, keepdims=True)
+                    top = jnp.max(top.astype(jnp.bfloat16), axis=1, keepdims=True)
+                    return top.astype(jnp.float32)
 
                 def weigh(i, top):
                     total = None

time: 142 us -> 143 us (level)
  no operation moved by 1% of the time
where the time goes in v4:
time: 143 us; the launch traced here: 141 us
  blocking collectives  45.1 us (32%)
  waiting for transfers between devices  39.3 us (27%)
  Pallas kernels  27.3 us (19%)
  starting transfers between devices  24.2 us (17%)
  other arithmetic  4.74 us (3%)
    all_to_all x1, blocking collectives, exchange(): lax.all_to_all(value, ('zh', 'dp'), split_axis=0, concat_axis=0, tiled=True)  45.1 us
    ppermute x4, waiting for transfers between devices, moved(): return lax.ppermute(value, ('dp', 'x', 'zh'), pairs)  20.2 us
    all_to_all x2, waiting for transfers between devices, exchange(): lax.all_to_all(value, ('zh', 'dp'), split_axis=0, concat_axis=0, tiled=True)  19.2 us
    pallas_call x1, Pallas kernels, attend(): pl.pallas_call(attend_kernel, in_specs=[SMEM] * 4 + [VMEM] + [HBM] * 7, o...  19 us
    all_to_all x2, starting transfers between devices, exchange(): lax.all_to_all(value, ('zh', 'dp'), split_axis=0, concat_axis=0, tiled=True)  14.7 us
    ppermute x4, starting transfers between devices, moved(): return lax.ppermute(value, ('dp', 'x', 'zh'), pairs)  9.51 us
    pallas_call x1, Pallas kernels, split_queries(): pl.pallas_call(split_queries_kernel, in_specs=[HBM, VMEM, VMEM], out_spec...  4.08 us
    mul x2, other arithmetic, tables(): jnp.sin(angles) * jnp.where(lane < HALF, -1.0, 1.0)  3.58 us
  transfers between devices with their start and end apart: 6, of which 4 were waited for; matrix products, arithmetic and copies ran while one was open for 3% of the time, Pallas kernels for 3%

profile of v4, /device:TPU:1, one launch (start us, length us, event | category | flops | bytes accessed | tf_op | source)
XLA Modules:
  0.0 141.3 jit_solution(9400899597859959350)
XLA Ops:
  0.0 2.0 %split_keys.1 = bf16[4,16,2,24,128]{4,3,2,1,0:T(8,128)(2,1)} custom-call(bf16[16,24,512]{2,1,0:T(8,128)(2,1)} %bitcast.20, bf16[16,24,512]{2,1,0:T(8,128)(2,1)} %bitcast.21), custom_call_target="tpu_custom_call" | custom-call | tf_op jit(solution)/shard_map/split_keys/pallas_call | solution.py:85
  2.0 9.6 %all-to-all-start.1 = ((bf16[32,2,2,24,128]{4,3,2,1,0:T(8,128)(2,1)}), bf16[32,2,2,24,128]{4,3,2,1,0:T(8,128)(2,1)S(1)}, u32[]{:S(2)}, u32[]{:S(2)}) async-start(bf16[32,2,2,24,128]{4,3,2,1,0:T(8,128)(2,1)} %bitcast.19), calls=%async_computation.1 | async-start | bytes 1572864 | tf_op jit(solution)/shard_map/all_to_all | solution.py:352
  11.7 0.1 add_convert_fusion.1
  11.8 0.1 add_convert_fusion
  11.8 0.8 fusion.1
  12.6 2.8 %fusion = (f32[2,768,128]{2,1,0:T(8,128)S(1)}, f32[2,768,128]{2,1,0:T(8,128)S(1)}) fusion(f32[128]{0:T(128)S(1)} %get-tuple-element.27, f32[128]{0:T(128)S(1)} %get-tuple-element.28, f32[2,768]{1,0:T(2,128)S(1)} %add_convert_fusion.1), kind=kLoop, calls=%fused_computation.2 | loop fusion | flops 393216 | bytes 1580032 | tf_op jit(solution)/shard_map/mul | solution.py:374
  15.4 4.1 %split_queries.1 = bf16[4,16,8,24,128]{4,3,2,1,0:T(8,128)(2,1)} custom-call(bf16[16,24,4096]{2,1,0:T(8,128)(2,1)} %bitcast.18, f32[16,24,128]{2,1,0:T(8,128)S(1)} %get-tuple-element.13.cos_ref, f32[16,24,128]{2,1,0:T(8,128)S(1)} %get-tuple-element.14.sin_ref), custom_call_target="tpu_custom_call" | custom-call | flops 10000000 | bytes 6500000 | tf_op jit(solution)/shard_map/split_queries/pallas_call | solution.py:129
  19.5 6.3 %all-to-all-done.1.in_ref = bf16[32,2,2,24,128]{4,3,2,1,0:T(8,128)(2,1)S(1)} async-done(((bf16[32,2,2,24,128]{4,3,2,1,0:T(8,128)(2,1)}), bf16[32,2,2,24,128]{4,3,2,1,0:T(8,128)(2,1)S(1)}, u32[]{:S(2)}, u32[]{:S(2)}) %all-to-all-start.1) | async-done | bytes 786464 | tf_op jit(solution)/shard_map/all_to_all | solution.py:352
  25.9 0.0 copy-start.6
  25.9 5.1 %all-to-all-start = ((bf16[32,2,8,24,128]{4,3,2,1,0:T(8,128)(2,1)}), bf16[32,2,8,24,128]{4,3,2,1,0:T(8,128)(2,1)}, u32[]{:S(2)}, u32[]{:S(2)}) async-start(bf16[32,2,8,24,128]{4,3,2,1,0:T(8,128)(2,1)} %bitcast.17), calls=%async_computation | async-start | bytes 6291456 | tf_op jit(solution)/shard_map/all_to_all | solution.py:352
  31.0 0.0 copy-done.6
  31.0 0.1 select_reduce_fusion
  31.1 0.1 broadcast_add_fusion
  31.2 0.2 select_reduce_fusion.2
  31.4 0.1 subtract_add_fusion
  31.4 0.1 sub.37
  31.5 0.3 turn_keys.1
  31.9 0.0 copy-start
  31.9 0.0 copy-start.1
  31.9 1.3 collective-permute-start
  33.2 3.1 %collective-permute-start.1 = (bf16[768,256]{1,0:T(8,128)(2,1)S(1)}, bf16[768,256]{1,0:T(8,128)(2,1)S(1)}, u32[]{:S(2)}, u32[]{:S(2)}) collective-permute-start(bf16[768,256]{1,0:T(8,128)(2,1)S(1)} %get-tuple-element.18.own1), channel_id=1, source_target_pairs={{0,2},{1,3},{2,4},{3,5},{4,6},{5,7},{6,8},{7,9},{8,10},{9,11},{10,... | collective-permute-start | bytes 1179656 | tf_op jit(solution)/shard_map/ppermute | solution.py:366
  36.3 0.2 convert_reduce_fusion
  36.5 0.1 slice.3
  36.6 0.1 select_reduce_fusion.1.order_ref
  36.7 1.5 %collective-permute-start.2 = (bf16[384,256]{1,0:T(8,128)(2,1)S(1)}, bf16[384,256]{1,0:T(8,128)(2,1)S(1)}, u32[]{:S(2)}, u32[]{:S(2)}) collective-permute-start(bf16[384,256]{1,0:T(8,128)(2,1)S(1)} %get-tuple-element.19), channel_id=1, source_target_pairs={{0,4},{1,5},{2,6},{3,7},{4,0},{5,1},{6,2},{7,3},{8,12},{9,13},{10,... | collective-permute-start | bytes 589832 | tf_op jit(solution)/shard_map/ppermute | solution.py:366
  38.2 3.6 %collective-permute-start.3 = (bf16[384,256]{1,0:T(8,128)(2,1)S(1)}, bf16[384,256]{1,0:T(8,128)(2,1)S(1)}, u32[]{:S(2)}, u32[]{:S(2)}) collective-permute-start(bf16[384,256]{1,0:T(8,128)(2,1)S(1)} %get-tuple-element.20), channel_id=1, source_target_pairs={{0,4},{1,5},{2,6},{3,7},{4,8},{5,9},{6,10},{7,11},{8,12},{9,13},{1... | collective-permute-start | bytes 589832 | tf_op jit(solution)/shard_map/ppermute | solution.py:366
  41.8 0.1 add_convert_fusion.2.flag_ref
  41.9 0.2 select_reduce_fusion.3.most_ref
  42.1 15.1 %collective-permute-done.2.far0 = bf16[384,256]{1,0:T(8,128)(2,1)S(1)} collective-permute-done((bf16[384,256]{1,0:T(8,128)(2,1)S(1)}, bf16[384,256]{1,0:T(8,128)(2,1)S(1)}, u32[]{:S(2)}, u32[]{:S(2)}) %collective-permute-start.2) | collective-permute-done | bytes 196640 | tf_op jit(solution)/shard_map/ppermute | solution.py:366
  57.2 0.0 copy-start.4
  57.2 5.1 %collective-permute-done.3.far1 = bf16[384,256]{1,0:T(8,128)(2,1)S(1)} collective-permute-done((bf16[384,256]{1,0:T(8,128)(2,1)S(1)}, bf16[384,256]{1,0:T(8,128)(2,1)S(1)}, u32[]{:S(2)}, u32[]{:S(2)}) %collective-permute-start.3) | collective-permute-done | bytes 196640 | tf_op jit(solution)/shard_map/ppermute | solution.py:366
  62.2 0.0 copy-start.5
  62.3 0.0 collective-permute-done.near0
  62.3 0.0 copy-start.2
  62.3 0.0 collective-permute-done.1.near1
  62.3 0.0 copy-start.3
  62.3 12.8 %all-to-all-done = bf16[32,2,8,24,128]{4,3,2,1,0:T(8,128)(2,1)} async-done(((bf16[32,2,8,24,128]{4,3,2,1,0:T(8,128)(2,1)}), bf16[32,2,8,24,128]{4,3,2,1,0:T(8,128)(2,1)}, u32[]{:S(2)}, u32[]{:S(2)}) %all-to-all-start) | async-done | bytes 3145760 | tf_op jit(solution)/shard_map/all_to_all | solution.py:352
  75.1 0.0 copy-done
  75.1 0.0 copy-done.1
  75.1 0.0 copy-done.4
  75.1 0.0 copy-done.5
  75.1 0.0 copy-done.2
  75.1 0.0 copy-done.3
  75.1 19.0 %attend.1 = bf16[32,2,192,128]{3,2,1,0:T(8,128)(2,1)S(1)} custom-call(s32[32]{0:T(128)S(1)} %select_reduce_fusion.1.order_ref, s32[8]{0:T(128)S(1)} %select_reduce_fusion.3.most_ref, s32[2]{0:T(128)S(1)} %get-tuple-element.21.base_ref, s32[2]{0:T(128)S(1)} %add_convert_fusion.2.flag_ref, s32[1,128]{1,0:T(1,128)S(1)} %bitcast.16, ...), custom_call_target="tpu_custom_call" | custom-call | flops 8000000000 | bytes 10000000 | tf_op jit(solution)/shard_map/attend/pallas_call | solution.py:327
  94.2 45.1 %all_to_all.15 = bf16[32,2,8,24,128]{4,3,2,1,0:T(8,128)(2,1)S(1)} all-to-all(bf16[32,2,8,24,128]{4,3,2,1,0:T(8,128)(2,1)S(1)} %bitcast.15), channel_id=1, replica_groups=mesh['dp'=16,'x'=4,'zh'=2] {'zh','dp'}, dimensions={0} | all-to-all | bytes 6291456 | tf_op jit(solution)/shard_map/all_to_all | solution.py:352
  139.3 1.8 %join_heads.1 = bf16[16,24,4096]{2,1,0:T(8,128)(2,1)} custom-call(bf16[4,16,8,24,128]{4,3,2,1,0:T(8,128)(2,1)S(1)} %bitcast.14), custom_call_target="tpu_custom_call" | custom-call | tf_op jit(solution)/shard_map/join_heads/pallas_call | solution.py:169
  (7 shorter events, 0.0 us)
Async XLA Ops:
  2.0 23.8 %all-to-all-start.1 = ((bf16[32,2,2,24,128]{4,3,2,1,0:T(8,128)(2,1)}), bf16[32,2,2,24,128]{4,3,2,1,0:T(8,128)(2,1)S(1)}, u32[]{:S(2)}, u32[]{:S(2)}) async-start(bf16[32,2,2,24,128]{4,3,2,1,0:T(8,128)(2,1)} %bitcast.19), calls=%async_computation.1 | async-start | bytes 1572864 | tf_op jit(solution)/shard_map/all_to_all | solution.py:352
  25.9 5.1 %copy-start.6 = (s32[64]{0:T(128)S(1)}, s32[64]{0:T(128)}, u32[]{:S(2)}) copy-start(s32[64]{0:T(128)} %param.7) | copy-start | bytes 772
  25.9 49.2 %all-to-all-start = ((bf16[32,2,8,24,128]{4,3,2,1,0:T(8,128)(2,1)}), bf16[32,2,8,24,128]{4,3,2,1,0:T(8,128)(2,1)}, u32[]{:S(2)}, u32[]{:S(2)}) async-start(bf16[32,2,8,24,128]{4,3,2,1,0:T(8,128)(2,1)} %bitcast.17), calls=%async_computation | async-start | bytes 6291456 | tf_op jit(solution)/shard_map/all_to_all | solution.py:352
  31.9 43.2 %copy-start = (bf16[768,256]{1,0:T(8,128)(2,1)}, bf16[768,256]{1,0:T(8,128)(2,1)S(1)}, u32[]{:S(2)}) copy-start(bf16[768,256]{1,0:T(8,128)(2,1)S(1)} %get-tuple-element.17.own0) | copy-start | bytes 1179652
  31.9 43.2 %copy-start.1 = (bf16[768,256]{1,0:T(8,128)(2,1)}, bf16[768,256]{1,0:T(8,128)(2,1)S(1)}, u32[]{:S(2)}) copy-start(bf16[768,256]{1,0:T(8,128)(2,1)S(1)} %get-tuple-element.18.own1) | copy-start | bytes 1179652
  31.9 30.4 %collective-permute-start = (bf16[768,256]{1,0:T(8,128)(2,1)S(1)}, bf16[768,256]{1,0:T(8,128)(2,1)S(1)}, u32[]{:S(2)}, u32[]{:S(2)}) collective-permute-start(bf16[768,256]{1,0:T(8,128)(2,1)S(1)} %get-tuple-element.17.own0), channel_id=1, source_target_pairs={{0,2},{1,3},{2,4},{3,5},{4,6},{5,7},{6,0},{7,1},{8,10},{9,11},{10,... | collective-permute-start | bytes 1179656 | tf_op jit(solution)/shard_map/ppermute | solution.py:366
  33.2 29.1 %collective-permute-start.1 = (bf16[768,256]{1,0:T(8,128)(2,1)S(1)}, bf16[768,256]{1,0:T(8,128)(2,1)S(1)}, u32[]{:S(2)}, u32[]{:S(2)}) collective-permute-start(bf16[768,256]{1,0:T(8,128)(2,1)S(1)} %get-tuple-element.18.own1), channel_id=1, source_target_pairs={{0,2},{1,3},{2,4},{3,5},{4,6},{5,7},{6,8},{7,9},{8,10},{9,11},{10,... | collective-permute-start | bytes 1179656 | tf_op jit(solution)/shard_map/ppermute | solution.py:366
  36.7 20.5 %collective-permute-start.2 = (bf16[384,256]{1,0:T(8,128)(2,1)S(1)}, bf16[384,256]{1,0:T(8,128)(2,1)S(1)}, u32[]{:S(2)}, u32[]{:S(2)}) collective-permute-start(bf16[384,256]{1,0:T(8,128)(2,1)S(1)} %get-tuple-element.19), channel_id=1, source_target_pairs={{0,4},{1,5},{2,6},{3,7},{4,0},{5,1},{6,2},{7,3},{8,12},{9,13},{10,... | collective-permute-start | bytes 589832 | tf_op jit(solution)/shard_map/ppermute | solution.py:366
  38.2 24.0 %collective-permute-start.3 = (bf16[384,256]{1,0:T(8,128)(2,1)S(1)}, bf16[384,256]{1,0:T(8,128)(2,1)S(1)}, u32[]{:S(2)}, u32[]{:S(2)}) collective-permute-start(bf16[384,256]{1,0:T(8,128)(2,1)S(1)} %get-tuple-element.20), channel_id=1, source_target_pairs={{0,4},{1,5},{2,6},{3,7},{4,8},{5,9},{6,10},{7,11},{8,12},{9,13},{1... | collective-permute-start | bytes 589832 | tf_op jit(solution)/shard_map/ppermute | solution.py:366
  57.2 17.9 %copy-start.4 = (bf16[384,256]{1,0:T(8,128)(2,1)}, bf16[384,256]{1,0:T(8,128)(2,1)S(1)}, u32[]{:S(2)}) copy-start(bf16[384,256]{1,0:T(8,128)(2,1)S(1)} %collective-permute-done.2.far0) | copy-start | bytes 589828
  62.2 12.9 %copy-start.5 = (bf16[384,256]{1,0:T(8,128)(2,1)}, bf16[384,256]{1,0:T(8,128)(2,1)S(1)}, u32[]{:S(2)}) copy-start(bf16[384,256]{1,0:T(8,128)(2,1)S(1)} %collective-permute-done.3.far1) | copy-start | bytes 589828
  62.3 12.9 %copy-start.2 = (bf16[768,256]{1,0:T(8,128)(2,1)}, bf16[768,256]{1,0:T(8,128)(2,1)S(1)}, u32[]{:S(2)}) copy-start(bf16[768,256]{1,0:T(8,128)(2,1)S(1)} %collective-permute-done.near0) | copy-start | bytes 1179652
  62.3 12.9 %copy-start.3 = (bf16[768,256]{1,0:T(8,128)(2,1)}, bf16[768,256]{1,0:T(8,128)(2,1)S(1)}, u32[]{:S(2)}) copy-start(bf16[768,256]{1,0:T(8,128)(2,1)S(1)} %collective-permute-done.1.near1) | copy-start | bytes 1179652
